TPU v7x, 32 devices: a whole 2x2x4 slice. The times are simulated.
32 devices in a mesh: groups: 2 (over y), dap: 4 (over z), seq: 2 (over x), chan: 2 (over core).
Axes of the slice: x: 2, y: 2, z: 4, core: 2. Of those that a mesh axis runs over, the one named last changes fastest.
Arguments:
- alignment: bfloat16 [128, 96, 256], P(('groups', 'seq'), 'dap'), parts along dimension 0, may hold values from -8 to 8
- align_mask: int32 [128, 96], P('groups'), parts along dimension 0, may hold values from 0 to 1, as said below
- pair_mask: int32 [192, 96], P(('groups', 'dap')), parts along dimension 0, may hold values 0 or 1
- cotangent: bfloat16 [192, 96, 128], P(('groups', 'dap'), 'seq', 'chan'), parts along dimension 0, may hold values from -150 to 150
- left_weight: bfloat16 [256, 32], replicated, may hold values from -0.375 to 0.375
- right_weight: bfloat16 [256, 32], replicated, may hold values from -0.375 to 0.375
- out_weight: bfloat16 [1024, 128], P(None, 'chan'), may hold values from -0.1875 to 0.1875
Outputs:
- pair_update: bfloat16 [192, 96, 128], P(('groups', 'dap'), 'seq', 'chan'), parts along dimension 0
- grad_alignment: bfloat16 [128, 96, 256], P(('groups', 'seq'), 'dap'), parts along dimension 0
- grad_left_weight: float32 [512, 32], P('groups'), parts along dimension 0
- grad_right_weight: float32 [512, 32], P('groups'), parts along dimension 0
- grad_out_weight: float32 [2048, 128], P('groups', 'chan'), parts along dimension 0
There are 2 independent parts, one for each index of `groups`. A program takes and returns all parts, laid end to end along the dimension named above; an argument that names none is the same for every part. Nothing has to cross between parts.
Inputs may be any that keep to these rules, and one draw needn't show every extreme that they name: `align_mask`: entries are 0 or 1; the first sequence is 1 at every residue.
All inputs are finite; a program needn't handle non-finite values. No bound on the sum of `pair_mask` on one device may be relied on, other than what follows from the above.
Results may differ from a plain program's by a relative error of at most 0.0075.
Values may be sent and summed in bfloat16 or wider, within the bound.
A program may use at most 64 MiB of HBM per device.

v0:
```python
import math

import jax
import jax.numpy as jnp
from jax import lax
from jax.sharding import PartitionSpec as P

SBLK = 32


def layer_norm(values):
    center = values - jnp.mean(values, axis=-1, keepdims=True)
    variance = jnp.mean(center * center, axis=-1, keepdims=True)
    return center * lax.rsqrt(variance + 1e-05)


def outer_grad(grad_block, weight_full, outer_width):
    flat_grad = grad_block.reshape(-1, weight_full.shape[1])
    douter = lax.dot_general(
        flat_grad, weight_full, (((1,), (1,)), ((), ())), preferred_element_type=jnp.float32
    )
    return douter.astype(jnp.bfloat16).reshape(
        grad_block.shape[0], grad_block.shape[1], outer_width, outer_width
    )


def body(alignment, align_mask, pair_mask, cotangent, left_weight, right_weight, out_weight):
    seq_rows, res_rows, _ = alignment.shape
    outer_width = left_weight.shape[1]
    chan_width = out_weight.shape[1]
    total_res = res_rows * lax.axis_size("dap")
    col_width = total_res // lax.axis_size("seq")
    res_start = lax.axis_index("dap") * res_rows
    seq_start = lax.axis_index("seq") * seq_rows
    mask_float = align_mask.astype(jnp.float32)
    own_mask = lax.dynamic_slice(mask_float, (seq_start, res_start), (seq_rows, res_rows))
    mask_rows = lax.dynamic_slice_in_dim(mask_float, res_start, res_rows, 1)
    counts = jnp.dot(mask_rows.T, mask_float, precision=lax.Precision.HIGHEST)
    pair_scale = pair_mask.astype(jnp.float32) / (counts + 0.001)
    source = alignment.astype(jnp.float32)
    normed = layer_norm(source).astype(jnp.bfloat16)
    left_act = (
        own_mask[:, :, None] * jnp.dot(normed, left_weight, preferred_element_type=jnp.float32)
    ).astype(jnp.bfloat16)
    right_act = (
        own_mask[:, :, None] * jnp.dot(normed, right_weight, preferred_element_type=jnp.float32)
    ).astype(jnp.bfloat16)
    right_flat = lax.all_gather(
        right_act.reshape(seq_rows, res_rows * outer_width), "dap", axis=1, tiled=True
    )
    right_res = right_flat.reshape(seq_rows, total_res, outer_width)
    num_blocks = seq_rows // SBLK
    left_blocks = left_act.reshape(num_blocks, SBLK, res_rows, outer_width)
    right_blocks = right_res.reshape(num_blocks, SBLK, total_res, outer_width)
    col_block = math.gcd(128, total_res)
    num_cols = total_res // col_block

    def outer_block(offset):
        right_cols = lax.dynamic_slice_in_dim(right_blocks, offset, col_block, 2)
        outer_prod = jnp.einsum(
            "ksic,ksjd->kijcd", left_blocks, right_cols, preferred_element_type=jnp.float32
        ).astype(jnp.bfloat16)
        return outer_prod.reshape(num_blocks, res_rows * col_block, outer_width * outer_width)

    def forward_step(column_index, partials):
        offset = column_index * col_block
        projected = jnp.einsum(
            "kpf,fe->pe", outer_block(offset), out_weight, preferred_element_type=jnp.float32
        )
        return lax.dynamic_update_slice_in_dim(
            partials, projected.reshape(res_rows, col_block, chan_width), offset, 1
        )

    partials = lax.fori_loop(
        0, num_cols, forward_step, jnp.zeros((res_rows, total_res, chan_width), jnp.float32)
    )
    summed = lax.psum_scatter(partials, "seq", scatter_dimension=1, tiled=True)
    scale_cols = lax.dynamic_slice_in_dim(
        pair_scale, lax.axis_index("seq") * col_width, col_width, 1
    )
    pair_update = (summed * scale_cols[:, :, None]).astype(jnp.bfloat16)
    grad_cols = lax.all_gather(cotangent, "seq", axis=1, tiled=True)
    own_grad = (grad_cols.astype(jnp.float32) * pair_scale[:, :, None]).astype(jnp.bfloat16)

    def weight_step(column_index, wo_acc):
        offset = column_index * col_block
        own_cols = lax.dynamic_slice_in_dim(own_grad, offset, col_block, 1).reshape(
            res_rows * col_block, chan_width
        )
        return wo_acc + jnp.einsum(
            "kpf,pe->fe", outer_block(offset), own_cols, preferred_element_type=jnp.float32
        )

    wo_part = lax.fori_loop(
        0, num_cols, weight_step, jnp.zeros((outer_width * outer_width, chan_width), jnp.float32)
    )
    weight_full = lax.all_gather(out_weight, "chan", axis=1, tiled=True)
    half_width = total_res // lax.axis_size("chan")
    half_start = lax.axis_index("chan") * half_width
    half_block = math.gcd(128, half_width)
    num_half = half_width // half_block
    grad_half = lax.all_to_all(grad_cols, "chan", split_axis=1, concat_axis=2, tiled=True)
    scale_half = lax.dynamic_slice_in_dim(pair_scale, half_start, half_width, 1)
    scaled_half = (grad_half.astype(jnp.float32) * scale_half[:, :, None]).astype(jnp.bfloat16)

    def half_step(column_index, running):
        left_acc, right_acc = running
        offset = column_index * half_block
        right_cols = lax.dynamic_slice_in_dim(right_blocks, half_start + offset, half_block, 2)
        douter = outer_grad(
            lax.dynamic_slice_in_dim(scaled_half, offset, half_block, 1), weight_full, outer_width
        )
        left_acc = left_acc + jnp.einsum(
            "ijcd,ksjd->ksic", douter, right_cols, preferred_element_type=jnp.float32
        )
        right_term = jnp.einsum(
            "ijcd,ksic->ksjd", douter, left_blocks, preferred_element_type=jnp.float32
        )
        right_acc = lax.dynamic_update_slice_in_dim(right_acc, right_term, half_start + offset, 2)
        return (left_acc, right_acc)

    left_part, right_part = lax.fori_loop(
        0,
        num_half,
        half_step,
        (
            jnp.zeros((num_blocks, SBLK, res_rows, outer_width), jnp.float32),
            jnp.zeros((num_blocks, SBLK, total_res, outer_width), jnp.float32),
        ),
    )
    right_summed = lax.psum_scatter(
        right_part.reshape(seq_rows, total_res * outer_width),
        "dap",
        scatter_dimension=1,
        tiled=True,
    )
    right_part = right_summed.reshape(seq_rows, res_rows, outer_width)
    left_sum, right_sum = lax.psum(
        (left_part.reshape(seq_rows, res_rows, outer_width), right_part), "chan"
    )
    left_grad = (own_mask[:, :, None] * left_sum).astype(jnp.bfloat16)
    right_grad = (own_mask[:, :, None] * right_sum).astype(jnp.bfloat16)
    left_wpart = jnp.einsum("src,srd->cd", normed, left_grad, preferred_element_type=jnp.float32)
    right_wpart = jnp.einsum("src,srd->cd", normed, right_grad, preferred_element_type=jnp.float32)
    wo_total, left_total, right_total = lax.psum((wo_part, left_wpart, right_wpart), ("dap", "seq"))
    normed_grad = jnp.einsum(
        "srd,cd->src", left_grad, left_weight, preferred_element_type=jnp.float32
    )
    normed_grad = normed_grad + jnp.einsum(
        "srd,cd->src", right_grad, right_weight, preferred_element_type=jnp.float32
    )
    _, pullback = jax.vjp(layer_norm, source)
    grad_alignment = pullback(normed_grad)[0].astype(jnp.bfloat16)
    return (
        pair_update,
        grad_alignment,
        left_total / total_res,
        right_total / total_res,
        wo_total / total_res,
    )


def solution(mesh):
    placed = (
        P(("groups", "seq"), "dap", None),
        P("groups", None),
        P(("groups", "dap"), None),
        P(("groups", "dap"), "seq", "chan"),
        P(),
        P(),
        P(None, "chan"),
    )
    return jax.shard_map(
        body,
        mesh=mesh,
        in_specs=placed,
        out_specs=(
            P(("groups", "dap"), "seq", "chan"),
            P(("groups", "seq"), "dap", None),
            P("groups", None),
            P("groups", None),
            P("groups", "chan"),
        ),
        check_vma=False,
    )
```

profile of v0, /device:TPU:0, one launch (start us, length us, event | category | flops | bytes accessed | tf_op | source)
XLA Modules:
  0.0 341.5 jit_solution(6278215451133081978)
XLA Ops:
  9.1 10.6 %all_gather.10 = bf16[24,96,64]{2,0,1:T(8,128)(2,1)S(1)} all-gather(bf16[24,48,64]{2,0,1:T(8,128)(2,1)S(1)} %copy.62), channel_id=1, replica_groups=mesh['groups'=2,'dap'=4,'seq'=2,'chan'=2] {'seq'}, dimensions={1}, use_global_device_ids=true | all-gather | bytes 442368 | tf_op jit(solution)/shard_map/all_gather | solution.py:82
  26.2 14.1 %all_gather.9 = bf16[32,3072]{1,0:T(8,128)(2,1)S(1)} all-gather(bf16[32,768]{1,0:T(8,128)(2,1)S(1)} %reshape.141), channel_id=1, replica_groups=mesh['groups'=2,'dap'=4,'seq'=2,'chan'=2] {'dap'}, dimensions={1}, use_global_device_ids=true | all-gather | bytes 245760 | tf_op jit(solution)/shard_map/all_gather | solution.py:48
  50.1 38.9 %while.44 = (s32[]{:T(128)}, f32[1,32,24,32]{3,1,2,0:T(8,128)}, f32[1,32,96,32]{1,3,2,0:T(8,128)}, s32[]{:T(128)}, bf16[1,32,96,32]{1,3,2,0:T(8,128)(2,1)}, /*in...) while((s32[]{:T(128)}, f32[1,32,24,32]{3,1,2,0:T(8,128)}, ...), condition=%wide.region_6.7_spmd.clone, body=%wide.region_5.0_spmd.clone.sunk | while | flops 151437312 | bytes 5423351 | solution.py:122
  94.1 19.8 %reduce-scatter.5.cloned.1.call-done = f32[32,768]{1,0:T(8,128)} async-done(((f32[32,3072]{1,0:T(8,128)}), f32[32,768]{1,0:T(8,128)}) %reduce-scatter.5.cloned.1.call-update) | async-done | bytes 98320 | tf_op jit(solution)/shard_map/reduce_scatter | solution.py:131
  115.9 74.0 %while.45 = (s32[]{:T(128)}, f32[1024,64]{0,1:T(8,128)}, bf16[1,32,96,32]{1,3,2,0:T(8,128)(2,1)S(1)}, bf16[1,32,24,32]{3,1,2,0:T(8,128)(2,1)S(1)}, bf16[24,96,64...) while((s32[]{:T(128)}, f32[1024,64]{0,1:T(8,128)}, ...), condition=%wide.region_15.0_spmd.clone, body=%wide.region_14.0_spmd.clone.sunk | while | flops 151912448 | bytes 10911909 | solution.py:94
  116.0 4.4 %convert_bitcast_fusion.6 = bf16[1,24,32,32,32]{3,4,1,2,0:T(8,128)(2,1)} fusion(bf16[1,32,96,32]{1,3,2,0:T(8,128)(2,1)S(1)} %get-tuple-element.697, s32[]{:T(128)S(6)} %select_n.58, bf16[1,32,24,32]{3,1,2,0:T(8,128)(2,1)S(1)} %get-tuple-element.698), kind=kOutput, calls=%fused_computation.17.clone.1 | convolution fusion | flops 51118080 | bytes 2031620 | tf_op jit(solution)/shard_map/while/body/eval_jaxpr/ksic,ksjd->kijcd/dot_general | solution.py:60
  120.4 8.7 %copy.85 = bf16[1,24,32,32,32]{4,3,2,1,0:T(8,128)(2,1)} copy(bf16[1,24,32,32,32]{3,4,1,2,0:T(8,128)(2,1)} %convert_bitcast_fusion.6) | data formatting | bytes 3145728 | tf_op jit(solution)/shard_map/while/body/eval_jaxpr/convert_element_type | solution.py:62
  129.1 8.8 %reduce_sum.65 = bf16[768,1024]{1,0:T(8,128)(2,1)S(1)} reshape(bf16[1,24,32,32,32]{4,3,2,1,0:T(8,128)(2,1)} %copy.85) | data formatting | bytes 3145728 | tf_op jit(solution)/shard_map/while/body/eval_jaxpr/kpf,pe->fe/reduce_sum | solution.py:90
  140.1 4.4 %convert_bitcast_fusion.6 = bf16[1,24,32,32,32]{3,4,1,2,0:T(8,128)(2,1)} fusion(bf16[1,32,96,32]{1,3,2,0:T(8,128)(2,1)S(1)} %get-tuple-element.697, s32[]{:T(128)S(6)} %select_n.58, bf16[1,32,24,32]{3,1,2,0:T(8,128)(2,1)S(1)} %get-tuple-element.698), kind=kOutput, calls=%fused_computation.17.clone.1 | convolution fusion | flops 51118080 | bytes 2031620 | tf_op jit(solution)/shard_map/while/body/eval_jaxpr/ksic,ksjd->kijcd/dot_general | solution.py:60
  144.5 8.7 %copy.85 = bf16[1,24,32,32,32]{4,3,2,1,0:T(8,128)(2,1)} copy(bf16[1,24,32,32,32]{3,4,1,2,0:T(8,128)(2,1)} %convert_bitcast_fusion.6) | data formatting | bytes 3145728 | tf_op jit(solution)/shard_map/while/body/eval_jaxpr/convert_element_type | solution.py:62
  153.2 8.8 %reduce_sum.65 = bf16[768,1024]{1,0:T(8,128)(2,1)S(1)} reshape(bf16[1,24,32,32,32]{4,3,2,1,0:T(8,128)(2,1)} %copy.85) | data formatting | bytes 3145728 | tf_op jit(solution)/shard_map/while/body/eval_jaxpr/kpf,pe->fe/reduce_sum | solution.py:90
  165.0 4.4 %convert_bitcast_fusion.6 = bf16[1,24,32,32,32]{3,4,1,2,0:T(8,128)(2,1)} fusion(bf16[1,32,96,32]{1,3,2,0:T(8,128)(2,1)S(1)} %get-tuple-element.697, s32[]{:T(128)S(6)} %select_n.58, bf16[1,32,24,32]{3,1,2,0:T(8,128)(2,1)S(1)} %get-tuple-element.698), kind=kOutput, calls=%fused_computation.17.clone.1 | convolution fusion | flops 51118080 | bytes 2031620 | tf_op jit(solution)/shard_map/while/body/eval_jaxpr/ksic,ksjd->kijcd/dot_general | solution.py:60
  169.4 8.7 %copy.85 = bf16[1,24,32,32,32]{4,3,2,1,0:T(8,128)(2,1)} copy(bf16[1,24,32,32,32]{3,4,1,2,0:T(8,128)(2,1)} %convert_bitcast_fusion.6) | data formatting | bytes 3145728 | tf_op jit(solution)/shard_map/while/body/eval_jaxpr/convert_element_type | solution.py:62
  178.1 8.8 %reduce_sum.65 = bf16[768,1024]{1,0:T(8,128)(2,1)S(1)} reshape(bf16[1,24,32,32,32]{4,3,2,1,0:T(8,128)(2,1)} %copy.85) | data formatting | bytes 3145728 | tf_op jit(solution)/shard_map/while/body/eval_jaxpr/kpf,pe->fe/reduce_sum | solution.py:90
  195.9 69.6 %while.43 = (s32[]{:T(128)}, f32[24,96,64]{2,1,0:T(8,128)}, bf16[1,32,96,32]{1,3,2,0:T(8,128)(2,1)S(1)}, bf16[1,32,24,32]{3,1,2,0:T(8,128)(2,1)S(1)}, bf16[1024,...) while((s32[]{:T(128)}, f32[24,96,64]{2,1,0:T(8,128)}, ...), condition=%wide.region_3.4_spmd, body=%wide.region_2.3_spmd.sunk | while | flops 151781376 | bytes 10420379 | solution.py:74
  195.9 4.4 %convert_bitcast_fusion.5 = bf16[1,24,32,32,32]{3,4,1,2,0:T(8,128)(2,1)} fusion(bf16[1,32,96,32]{1,3,2,0:T(8,128)(2,1)S(1)} %get-tuple-element.631, s32[]{:T(128)S(6)} %select_n.55, bf16[1,32,24,32]{3,1,2,0:T(8,128)(2,1)S(1)} %get-tuple-element.632), kind=kOutput, calls=%fused_computation.clone.1 | convolution fusion | flops 51118080 | bytes 2031620 | tf_op jit(solution)/shard_map/while/body/eval_jaxpr/ksic,ksjd->kijcd/dot_general | solution.py:60
  200.4 8.7 %copy.84 = bf16[1,24,32,32,32]{4,3,2,1,0:T(8,128)(2,1)} copy(bf16[1,24,32,32,32]{3,4,1,2,0:T(8,128)(2,1)} %convert_bitcast_fusion.5) | data formatting | bytes 3145728 | tf_op jit(solution)/shard_map/while/body/eval_jaxpr/convert_element_type | solution.py:62
  209.0 8.8 %dot_general.84 = bf16[24,32,1024]{2,1,0:T(8,128)(2,1)S(1)} reshape(bf16[1,24,32,32,32]{4,3,2,1,0:T(8,128)(2,1)} %copy.84) | data formatting | bytes 3145728 | tf_op jit(solution)/shard_map/while/body/eval_jaxpr/kpf,fe->pe/dot_general | solution.py:67
  219.1 4.4 %convert_bitcast_fusion.5 = bf16[1,24,32,32,32]{3,4,1,2,0:T(8,128)(2,1)} fusion(bf16[1,32,96,32]{1,3,2,0:T(8,128)(2,1)S(1)} %get-tuple-element.631, s32[]{:T(128)S(6)} %select_n.55, bf16[1,32,24,32]{3,1,2,0:T(8,128)(2,1)S(1)} %get-tuple-element.632), kind=kOutput, calls=%fused_computation.clone.1 | convolution fusion | flops 51118080 | bytes 2031620 | tf_op jit(solution)/shard_map/while/body/eval_jaxpr/ksic,ksjd->kijcd/dot_general | solution.py:60
  223.5 8.7 %copy.84 = bf16[1,24,32,32,32]{4,3,2,1,0:T(8,128)(2,1)} copy(bf16[1,24,32,32,32]{3,4,1,2,0:T(8,128)(2,1)} %convert_bitcast_fusion.5) | data formatting | bytes 3145728 | tf_op jit(solution)/shard_map/while/body/eval_jaxpr/convert_element_type | solution.py:62
  232.2 8.8 %dot_general.84 = bf16[24,32,1024]{2,1,0:T(8,128)(2,1)S(1)} reshape(bf16[1,24,32,32,32]{4,3,2,1,0:T(8,128)(2,1)} %copy.84) | data formatting | bytes 3145728 | tf_op jit(solution)/shard_map/while/body/eval_jaxpr/kpf,fe->pe/dot_general | solution.py:67
  246.7 8.7 %copy.84 = bf16[1,24,32,32,32]{4,3,2,1,0:T(8,128)(2,1)} copy(bf16[1,24,32,32,32]{3,4,1,2,0:T(8,128)(2,1)} %convert_bitcast_fusion.5) | data formatting | bytes 3145728 | tf_op jit(solution)/shard_map/while/body/eval_jaxpr/convert_element_type | solution.py:62
  255.4 8.8 %dot_general.84 = bf16[24,32,1024]{2,1,0:T(8,128)(2,1)S(1)} reshape(bf16[1,24,32,32,32]{4,3,2,1,0:T(8,128)(2,1)} %copy.84) | data formatting | bytes 3145728 | tf_op jit(solution)/shard_map/while/body/eval_jaxpr/kpf,fe->pe/dot_general | solution.py:67
  269.9 61.1 %all-reduce.8.cloned.1.call-done = (f32[256,32]{0,1:T(8,128)}, f32[256,32]{0,1:T(8,128)}) async-done(((f32[256,32]{0,1:T(8,128)}, f32[256,32]{0,1:T(8,128)}), (f32[256,32]{0,1:T(8,128)}, f32[256,32]{0,1:T(8,128)})) %all-reduce.8.cloned.1.call-update) | async-done | bytes 65552 | tf_op jit(solution)/shard_map/psum | solution.py:145
  (119 shorter events, 93.4 us)
Async XLA Ops:
  8.0 17.6 %copy-start = (bf16[256,32]{0,1:T(8,128)(2,1)S(1)}, bf16[256,32]{0,1:T(8,128)(2,1)}, u32[]{:S(2)}) copy-start(bf16[256,32]{0,1:T(8,128)(2,1)} %param.18) | copy-start | bytes 49156
  8.0 16.4 %copy-start.13 = (s32[64,96]{1,0:T(8,128)S(1)}, s32[64,96]{1,0:T(8,128)}, u32[]{:S(2)}) copy-start(s32[64,96]{1,0:T(8,128)} %param.14) | copy-start | bytes 73732
  8.0 16.4 %copy-start.3 = (bf16[32,24,256]{2,1,0:T(8,128)(2,1)S(1)}, bf16[32,24,256]{2,1,0:T(8,128)(2,1)}, u32[]{:S(2)}) copy-start(bf16[32,24,256]{2,1,0:T(8,128)(2,1)} %param.13) | copy-start | bytes 1179652
  19.7 6.3 %copy-start.5 = (bf16[24,96,64]{2,0,1:T(8,128)(2,1)}, bf16[24,96,64]{2,0,1:T(8,128)(2,1)S(1)}, u32[]{:S(2)}) copy-start(bf16[24,96,64]{2,0,1:T(8,128)(2,1)S(1)} %all_gather.10) | copy-start | bytes 884740
  20.9 21.3 %all-to-all-start = ((bf16[2,2,36864]{2,1,0:T(2,128)(2,1)}), bf16[2,2,36864]{2,1,0:T(2,128)(2,1)S(1)}, u32[]{:S(2)}, u32[]{:S(2)}) async-start(bf16[2,2,36864]{2,1,0:T(2,128)(2,1)} %reshape.168), calls=%async_computation.1 | async-start | bytes 589824 | tf_op jit(solution)/shard_map/all_to_all | solution.py:102
  24.4 89.5 %reduce-scatter.5.cloned.1.call-start = ((), (), s32[]{:S(2)}) async-start(), calls=%async_computation.4 | async-start | bytes 491520 | tf_op jit(solution)/shard_map/reduce_scatter | solution.py:131
  24.6 16.8 %copy-start.14 = (bf16[256,32]{0,1:T(8,128)(2,1)S(1)}, bf16[256,32]{0,1:T(8,128)(2,1)}, u32[]{:S(2)}) copy-start(bf16[256,32]{0,1:T(8,128)(2,1)} %param.17) | copy-start | bytes 49156
  25.0 0.6 copy-start.10
  26.0 15.9 %copy-start.16 = (s32[24,96]{1,0:T(8,128)S(1)}, s32[24,96]{1,0:T(8,128)}, u32[]{:S(2)}) copy-start(s32[24,96]{1,0:T(8,128)} %param.15) | copy-start | bytes 27652
  42.7 1.6 copy-start.7
  89.0 2.9 copy-start.2
  89.0 3.9 %copy-start.6 = (bf16[24,96,64]{2,0,1:T(8,128)(2,1)S(1)}, bf16[24,96,64]{2,0,1:T(8,128)(2,1)}, u32[]{:S(2)}) copy-start(bf16[24,96,64]{2,0,1:T(8,128)(2,1)} %copy-done.5) | copy-start | bytes 884740
  91.7 98.4 %all-reduce.10.cloned.1.call-start = ((), (), s32[]{:S(2)}) async-start(), calls=%async_computation.7 | async-start | bytes 1572864 | tf_op jit(solution)/shard_map/psum | solution.py:138
  91.8 24.1 %copy-start.1 = (bf16[1,32,96,32]{1,3,2,0:T(8,128)(2,1)S(1)}, bf16[1,32,96,32]{1,3,2,0:T(8,128)(2,1)}, u32[]{:S(2)}) copy-start(bf16[1,32,96,32]{1,3,2,0:T(8,128)(2,1)} %get-tuple-element.717) | copy-start | bytes 589828
  115.7 149.9 %all-reduce.6.cloned.1.call-start = ((), (), s32[]{:S(2)}) async-start(), calls=%async_computation.5 | async-start | bytes 524288 | tf_op jit(solution)/shard_map/psum | solution.py:145
  115.9 74.1 %copy-start.4 = (bf16[32,24,256]{2,1,0:T(8,128)(2,1)S(1)}, bf16[32,24,256]{2,1,0:T(8,128)(2,1)}, u32[]{:S(2)}) copy-start(bf16[32,24,256]{2,1,0:T(8,128)(2,1)} %param.13) | copy-start | bytes 1179652
  190.0 141.0 %all-reduce.8.cloned.1.call-start = ((), (), s32[]{:S(2)}) async-start(), calls=%async_computation.6 | async-start | bytes 131072 | tf_op jit(solution)/shard_map/psum | solution.py:145
  194.6 137.8 %reduce-scatter.3.cloned.1.call-start = ((), (), s32[]{:S(2)}) async-start(), calls=%async_computation.3 | async-start | bytes 1769472 | tf_op jit(solution)/shard_map/reduce_scatter | solution.py:77
  265.5 1.8 copy-start.9
  265.5 1.8 copy-start.15
  265.5 2.1 copy-start.8
  267.3 0.8 copy-start.11
  268.1 64.3 %copy-start.12 = (f32[24,48]{1,0:T(8,128)S(1)}, f32[24,48]{1,0:T(8,128)}, u32[]{:S(2)}) copy-start(f32[24,48]{1,0:T(8,128)} %get-tuple-element.495) | copy-start | bytes 13828
Sparse Core Ops, SparseCore 0:
  91.8 22.0 reduce-scatter.4
  116.8 17.5 all-reduce.9
  190.1 68.8 all-reduce.5
  262.9 68.0 all-reduce.7
Sparse Core Ops, SparseCore 1:
  265.6 20.0 reduce-scatter.2
where the time goes:
time: 344 us; the launch traced here: 342 us
  local copies, waits for them, and re-layouts  137 us (40%)
  waiting for transfers between devices  81 us (24%)
  matrix products  67.2 us (20%)
  blocking collectives  26.7 us (8%)
  between operations  15.6 us (5%)
  other arithmetic  9.65 us (3%)
  starting transfers between devices  3.84 us (1%)
    psum x2, waiting for transfers between devices, body(): lax.psum((wo_part, left_wpart, right_wpart), ('dap', 'seq'))  61.1 us
    convert_element_type x6, local copies, waits for them, and re-layouts, outer_block(): outer_prod = jnp.einsum('ksic,ksjd->kijcd', left_blocks, right_cols, pref...  52 us
    dot_general x6, matrix products, outer_block(): jnp.einsum('ksic,ksjd->kijcd', left_blocks, right_cols, preferred_element...  26.6 us
    reduce_sum x3, local copies, waits for them, and re-layouts, weight_step(): jnp.einsum('kpf,pe->fe', outer_block(offset), own_cols, preferred_element...  26.3 us
    dot_general x3, local copies, waits for them, and re-layouts, forward_step(): jnp.einsum('kpf,fe->pe', outer_block(offset), out_weight, preferred_eleme...  26.3 us
    reduce_scatter x1, waiting for transfers between devices, body(): lax.psum_scatter(right_part.reshape(seq_rows, total_res * outer_width), '...  19.8 us
    all_gather x1, blocking collectives, body(): lax.all_gather(right_act.reshape(seq_rows, res_rows * outer_width), 'dap'...  14.1 us
    dot_general x3, matrix products, half_step(): jnp.einsum('ijcd,ksjd->ksic', douter, right_cols, preferred_element_type=...  13.1 us
  transfers between devices with their start and end apart: 6, of which 2 were waited for; matrix products, arithmetic and copies ran while one was open for 47% of the time, Pallas kernels for 0%

commit v1 on v0

v1 whole, which is shorter than its diff:
```python
import functools

import jax
import jax.numpy as jnp
from jax import lax
from jax.experimental import pallas as pl
from jax.experimental.pallas import tpu as pltpu
from jax.sharding import PartitionSpec as P

MESH = pl.DeviceIdType.MESH
VMEM_BYTES = 48 * 1024 * 1024
F32 = jnp.float32
BF16 = jnp.bfloat16


def layer_norm(values):
    center = values - jnp.mean(values, axis=-1, keepdims=True)
    variance = jnp.mean(center * center, axis=-1, keepdims=True)
    return center * lax.rsqrt(variance + 1e-05)


def dot(a, b, ca, cb):
    return lax.dot_general(a, b, (((ca,), (cb,)), ((), ())), preferred_element_type=F32)


def vmem_call(kernel, out_shape, scratch, num_in, collective_id=None):
    params = dict(vmem_limit_bytes=VMEM_BYTES)
    if collective_id is not None:
        params.update(collective_id=collective_id, has_side_effects=True)
    return pl.pallas_call(
        kernel,
        out_shape=out_shape,
        in_specs=[pl.BlockSpec(memory_space=pltpu.VMEM)] * num_in,
        out_specs=jax.tree.map(lambda _: pl.BlockSpec(memory_space=pltpu.VMEM), out_shape),
        scratch_shapes=scratch,
        compiler_params=pltpu.CompilerParams(**params),
    )


def plane_barrier(dap, seq):
    num = dap * seq
    me = lax.axis_index("dap") * seq + lax.axis_index("seq")
    barrier = pltpu.get_barrier_semaphore()
    for step in range(1, num):
        peer = lax.rem(me + step, num)
        pl.semaphore_signal(
            barrier,
            inc=1,
            device_id={"dap": peer // seq, "seq": lax.rem(peer, seq)},
            device_id_type=MESH,
        )
    return barrier, num - 1


def gather_kernel(dap, seq, left_ref, right_ref, lall_ref, rall_ref, lbuf, rbuf, lsend, lrecv, rsend, rrecv):
    per = dap // seq
    a = lax.axis_index("dap")
    q = lax.axis_index("seq")
    barrier, count = plane_barrier(dap, seq)
    pl.semaphore_wait(barrier, count)

    def right_copy(step):
        return pltpu.make_async_remote_copy(
            src_ref=right_ref,
            dst_ref=rbuf.at[lax.rem(a, per), q],
            send_sem=rsend.at[step],
            recv_sem=rrecv.at[lax.rem(a, per), q],
            device_id={"dap": lax.rem(a + step, dap), "seq": a // per},
            device_id_type=MESH,
        )

    def left_copy(step):
        return pltpu.make_async_remote_copy(
            src_ref=left_ref,
            dst_ref=lbuf.at[q],
            send_sem=lsend.at[step],
            recv_sem=lrecv.at[q],
            device_id={"seq": lax.rem(q + step, seq)},
            device_id_type=MESH,
        )

    own = a // per == q
    for step in range(1, dap):
        right_copy(step).start()
    pl.when(jnp.logical_not(own))(lambda: right_copy(0).start())
    for step in range(1, seq):
        left_copy(step).start()
    for src_q in range(seq):

        @pl.when(src_q != q)
        def _():
            pltpu.make_async_copy(lbuf.at[src_q], lbuf.at[src_q], lrecv.at[src_q]).wait()
            lall_ref[src_q] = lbuf[src_q]

        @pl.when(src_q == q)
        def _():
            lall_ref[src_q] = left_ref[...]

        for block in range(per):
            mine = jnp.logical_and(q * per + block == a, src_q == q)

            @pl.when(jnp.logical_not(mine))
            def _():
                pltpu.make_async_copy(
                    rbuf.at[block, src_q], rbuf.at[block, src_q], rrecv.at[block, src_q]
                ).wait()
                rall_ref[block, src_q] = rbuf[block, src_q]

            @pl.when(mine)
            def _():
                rall_ref[block, src_q] = right_ref[...]

    for step in range(1, dap):
        right_copy(step).wait_send()
    pl.when(jnp.logical_not(own))(lambda: right_copy(0).wait_send())
    for step in range(1, seq):
        left_copy(step).wait_send()


def main_kernel(left_ref, rt_ref, w_ref, cot_ref, sct_ref, pu_ref, dl_ref, drt_ref, dw_ref, sg, wbd, outer, dout):
    rows, cols, chan = cot_ref.shape
    width = 32
    pack = 128 // width
    groups = rows // pack
    for g in range(groups):
        parts = [
            cot_ref[g * pack + k].astype(F32) * sct_ref[:, g * pack + k : g * pack + k + 1]
            for k in range(pack)
        ]
        sg[g * cols : (g + 1) * cols, :] = jnp.concatenate(parts, axis=1).astype(BF16)
    row_part = lax.broadcasted_iota(jnp.int32, (128, pack * chan), 0) // width
    lane_part = lax.broadcasted_iota(jnp.int32, (128, pack * chan), 1) // chan
    diagonal = (row_part == lane_part).astype(F32).astype(BF16)
    for d in range(width):
        block = w_ref[d * width : (d + 1) * width, :]
        block = jnp.concatenate([block] * pack, axis=1)
        wbd[d * 128 : (d + 1) * 128, :] = jnp.concatenate([block] * pack, axis=0) * diagonal
    for ch in range(width // 8):
        piece = dot(sg[...], wbd[ch * 1024 : (ch + 1) * 1024, :], 1, 1).astype(BF16)
        for dd in range(8):
            at = (ch * 8 + dd) * cols
            for g in range(groups):
                dout[at : at + cols, g * 128 : (g + 1) * 128] = piece[
                    g * cols : (g + 1) * cols, dd * 128 : (dd + 1) * 128
                ]
    dl_ref[...] = dot(rt_ref[...], dout[...], 1, 0).astype(BF16)
    drt_ref[...] = dot(left_ref[...], dout[...], 1, 1).astype(BF16)
    for ch in range(width // 8):
        piece = dot(rt_ref[:, ch * 8 * cols : (ch + 1) * 8 * cols], left_ref[...], 0, 0)
        piece = piece.astype(BF16)
        for dd in range(8):
            at = (ch * 8 + dd) * 128
            for g in range(groups):
                outer[g * cols : (g + 1) * cols, at : at + 128] = piece[
                    dd * cols : (dd + 1) * cols, g * 128 : (g + 1) * 128
                ]
    lane_of = lax.broadcasted_iota(jnp.int32, (chan, 128), 1) // width
    for ch in range(width // pack):
        wide = dot(sg[...], outer[:, ch * pack * 128 : (ch + 1) * pack * 128], 0, 0)
        total = jnp.zeros((chan, 128), F32)
        for d in range(pack):
            part = jnp.zeros((chan, 128), F32)
            for k in range(pack):
                part = jnp.where(
                    lane_of == k,
                    wide[k * chan : (k + 1) * chan, d * 128 : (d + 1) * 128],
                    part,
                )
            part = part + pltpu.roll(part, 64, 1)
            part = part + pltpu.roll(part, 32, 1)
            total = jnp.where(lane_of == d, part, total)
        dw_ref[ch] = total.astype(BF16)
    projected = dot(outer[...], wbd[...], 1, 0)
    for g in range(groups):
        for k in range(pack):
            i = g * pack + k
            pu_ref[i] = (
                projected[g * cols : (g + 1) * cols, k * chan : (k + 1) * chan]
                * sct_ref[:, i : i + 1]
            ).astype(BF16)


def reduce_kernel(
    dap, seq, dl_ref, dr_ref, wo_ref, lg_ref, rg_ref, wot_ref,
    l1, r1, l2, r2, lin, rin, pair, wrecv, wall,
    csend, crecv, lsend, lrecv, rsend, rrecv, wsend, wrsem, gsend, grecv,
):
    per = dap // seq
    num = dap * seq
    a = lax.axis_index("dap")
    q = lax.axis_index("seq")
    h = lax.axis_index("chan")
    other = 1 - h
    me = a * seq + q
    barrier, count = plane_barrier(dap, seq)
    pl.semaphore_signal(barrier, inc=1, device_id={"chan": other}, device_id_type=MESH)
    pl.semaphore_wait(barrier, count + 1)

    def core_copy(src, dst, sem):
        return pltpu.make_async_remote_copy(
            src_ref=src, dst_ref=dst, send_sem=csend.at[sem], recv_sem=crecv.at[sem],
            device_id={"chan": other}, device_id_type=MESH,
        )

    def plane_copy(src, dst, send, recv, peer_a, peer_q):
        return pltpu.make_async_remote_copy(
            src_ref=src, dst_ref=dst, send_sem=send, recv_sem=recv,
            device_id={"dap": peer_a, "seq": peer_q}, device_id_type=MESH,
        )

    left_core = core_copy(dl_ref.at[other], l1, 0)
    right_core = core_copy(dr_ref.at[other], r1, 1)
    left_core.start()
    right_core.start()

    def scatter(step):
        peer = lax.rem(me + step, num)
        return plane_copy(
            wo_ref.at[peer], wrecv.at[step], wsend.at[step], wrsem.at[step],
            peer // seq, lax.rem(peer, seq),
        )

    def regather(step):
        peer = lax.rem(me + step, num)
        return plane_copy(
            wall.at[me], wall.at[me], gsend.at[step], grecv.at[me],
            peer // seq, lax.rem(peer, seq),
        )

    for step in range(1, num):
        scatter(step).start()

    def left_out(dest_q):
        return plane_copy(l2.at[dest_q], lin.at[q], lsend.at[dest_q], lrecv.at[q], a, dest_q)

    def right_out(block, dest_q):
        return plane_copy(
            r2.at[block, dest_q], rin.at[a], rsend.at[block, dest_q], rrecv.at[a],
            q * per + block, dest_q,
        )

    def is_me(block, dest_q):
        return jnp.logical_and(q * per + block == a, dest_q == q)

    right_core.wait()
    for block in range(per):
        for dest_q in range(seq):
            r2[block, dest_q] = (
                dr_ref[h, block, dest_q].astype(F32) + r1[block, dest_q].astype(F32)
            ).astype(BF16)

            @pl.when(jnp.logical_not(is_me(block, dest_q)))
            def _():
                right_out(block, dest_q).start()

    left_core.wait()
    for dest_q in range(seq):
        l2[dest_q] = (dl_ref[h, dest_q].astype(F32) + l1[dest_q].astype(F32)).astype(BF16)

        @pl.when(dest_q != q)
        def _():
            left_out(dest_q).start()

    def arrived(buf, sem):
        pltpu.make_async_copy(buf, buf, sem).wait()

    left_sum = l2[q].astype(F32)
    for step in range(1, seq):
        src_q = lax.rem(q + step, seq)
        arrived(lin.at[src_q], lrecv.at[src_q])
        left_sum = left_sum + lin[src_q].astype(F32)
    pair[h, 0] = left_sum.astype(BF16)

    own = a // per == q

    @pl.when(own)
    def _():
        rin[a] = r2[lax.rem(a, per), q]

    @pl.when(jnp.logical_not(own))
    def _():
        arrived(rin.at[a], rrecv.at[a])

    right_sum = rin[a].astype(F32)
    for step in range(1, dap):
        src_a = lax.rem(a + step, dap)
        arrived(rin.at[src_a], rrecv.at[src_a])
        right_sum = right_sum + rin[src_a].astype(F32)
    pair[h, 1] = right_sum.astype(BF16)
    final = core_copy(pair.at[h], pair.at[h], 2)
    final.start()

    wo_sum = wo_ref[me].astype(F32)
    for step in range(1, num):
        arrived(wrecv.at[step], wrsem.at[step])
        wo_sum = wo_sum + wrecv[step].astype(F32)
    wall[me] = wo_sum.astype(BF16)
    for step in range(1, num):
        regather(step).start()

    final.wait_send()
    arrived(pair.at[other], crecv.at[2])
    for half in range(2):
        lg_ref[half] = pair[half, 0]
        rg_ref[half] = pair[half, 1]
    for step in range(1, num):
        src = lax.rem(me + step, num)
        arrived(wall.at[src], grecv.at[src])
    wot_ref[...] = wall[...]

    for step in range(1, num):
        scatter(step).wait_send()
        regather(step).wait_send()
    for dest_q in range(seq):

        @pl.when(dest_q != q)
        def _():
            left_out(dest_q).wait_send()

        for block in range(per):

            @pl.when(jnp.logical_not(is_me(block, dest_q)))
            def _():
                right_out(block, dest_q).wait_send()


def total_kernel(dap, seq, part_ref, total_ref, own, inbox, send, recv):
    num = dap * seq
    me = lax.axis_index("dap") * seq + lax.axis_index("seq")
    barrier, count = plane_barrier(dap, seq)
    own[...] = part_ref[...].astype(BF16)
    pl.semaphore_wait(barrier, count)

    def copy(step):
        peer = lax.rem(me + step, num)
        return pltpu.make_async_remote_copy(
            src_ref=own, dst_ref=inbox.at[step], send_sem=send.at[step], recv_sem=recv.at[step],
            device_id={"dap": peer // seq, "seq": lax.rem(peer, seq)}, device_id_type=MESH,
        )

    for step in range(1, num):
        copy(step).start()
    inbox[0] = own[...]
    for step in range(1, num):
        copy(step).wait()
    total = jnp.zeros(part_ref.shape, F32)
    for source in range(num):
        total = total + inbox[lax.rem(me - source + num, num)].astype(F32)
    total_ref[...] = total


def body(alignment, align_mask, pair_mask, cotangent, left_weight, right_weight, out_weight):
    seqs, rows, chans = alignment.shape
    width = left_weight.shape[1]
    chan = out_weight.shape[1]
    dap, seq = lax.axis_size("dap"), lax.axis_size("seq")
    per, num = dap // seq, dap * seq
    total_res, all_seqs = rows * dap, seqs * seq
    cols = total_res // seq
    a, q = lax.axis_index("dap"), lax.axis_index("seq")
    half = seqs // 2
    flat = rows * width

    mask_bf = align_mask.astype(BF16)
    own_mask = lax.dynamic_slice(align_mask, (q * seqs, a * rows), (seqs, rows)).astype(F32)
    mask_rows = lax.dynamic_slice_in_dim(mask_bf, a * rows, rows, 1)
    mask_cols = lax.dynamic_slice_in_dim(mask_bf, q * cols, cols, 1)
    counts = dot(mask_cols, mask_rows, 0, 0)
    own_pairs = lax.dynamic_slice_in_dim(pair_mask, q * cols, cols, 1)
    scale_t = own_pairs.T.astype(F32) / (counts + 0.001)

    source = alignment.astype(F32)
    normed = layer_norm(source).astype(BF16)
    both_weights = jnp.concatenate([left_weight, right_weight], axis=1)
    act = dot(normed.reshape(seqs * rows, chans), both_weights, 1, 0)
    act = (own_mask[:, :, None] * act.reshape(seqs, rows, 2 * width)).astype(BF16)
    left = act[:, :, :width].reshape(seqs, flat)
    right = act[:, :, width:].transpose(0, 2, 1).reshape(seqs, flat)

    dma = pltpu.SemaphoreType.DMA
    shape = jax.ShapeDtypeStruct
    left_all, right_all = vmem_call(
        functools.partial(gather_kernel, dap, seq),
        (shape((seq, seqs, flat), BF16), shape((per, seq, seqs, flat), BF16)),
        [
            pltpu.VMEM((seq, seqs, flat), BF16),
            pltpu.VMEM((per, seq, seqs, flat), BF16),
            dma((seq,)), dma((seq,)), dma((dap,)), dma((per, seq)),
        ],
        2,
        0,
    )(left, right)
    left_all = left_all.reshape(all_seqs, flat)
    right_t = right_all.reshape(per, seq, seqs, width, rows).transpose(1, 2, 3, 0, 4)
    right_t = right_t.reshape(all_seqs, width * cols)
    w_dc = out_weight.reshape(width, width, chan).transpose(1, 0, 2).reshape(width * width, chan)

    groups = rows // 4
    pair_update, dl, drt, dw = vmem_call(
        main_kernel,
        (
            shape((rows, cols, chan), BF16),
            shape((all_seqs, flat), BF16),
            shape((all_seqs, width * cols), BF16),
            shape((width // 4, chan, 128), BF16),
        ),
        [
            pltpu.VMEM((groups * cols, 4 * chan), BF16),
            pltpu.VMEM((width * 128, 4 * chan), BF16),
            pltpu.VMEM((groups * cols, width * 128), BF16),
            pltpu.VMEM((width * cols, groups * 128), BF16),
        ],
        5,
    )(left_all, right_t, w_dc, cotangent, scale_t)

    dl = dl.reshape(seq, 2, half, flat).transpose(1, 0, 2, 3)
    dr = drt.reshape(seq, 2, half, width, per, rows).transpose(1, 4, 0, 2, 5, 3)
    dr = dr.reshape(2, per, seq, half, flat)
    wrows = width // 4 * chan // num
    lg, rg, wo = vmem_call(
        functools.partial(reduce_kernel, dap, seq),
        (
            shape((2, half, flat), BF16),
            shape((2, half, flat), BF16),
            shape((num, wrows, 128), BF16),
        ),
        [
            pltpu.VMEM((seq, half, flat), BF16),
            pltpu.VMEM((per, seq, half, flat), BF16),
            pltpu.VMEM((seq, half, flat), BF16),
            pltpu.VMEM((per, seq, half, flat), BF16),
            pltpu.VMEM((seq, half, flat), BF16),
            pltpu.VMEM((dap, half, flat), BF16),
            pltpu.VMEM((2, 2, half, flat), BF16),
            pltpu.VMEM((num, wrows, 128), BF16),
            pltpu.VMEM((num, wrows, 128), BF16),
            dma((3,)), dma((3,)),
            dma((seq,)), dma((seq,)),
            dma((per, seq)), dma((dap,)),
            dma((num,)), dma((num,)),
            dma((num,)), dma((num,)),
        ],
        3,
        1,
    )(dl, dr, dw.reshape(num, wrows, 128))
    grads = jnp.concatenate(
        [lg.reshape(seqs, rows, width), rg.reshape(seqs, rows, width)], axis=2
    )
    grads = (grads.astype(F32) * own_mask[:, :, None]).astype(BF16).reshape(seqs * rows, 2 * width)
    weight_part = dot(grads, normed.reshape(seqs * rows, chans), 0, 0)
    weight_total = vmem_call(
        functools.partial(total_kernel, dap, seq),
        shape((2 * width, chans), F32),
        [
            pltpu.VMEM((2 * width, chans), BF16),
            pltpu.VMEM((num, 2 * width, chans), BF16),
            dma((num,)), dma((num,)),
        ],
        1,
        2,
    )(weight_part)
    normed_grad = dot(grads, both_weights, 1, 1).reshape(seqs, rows, chans)
    _, pullback = jax.vjp(layer_norm, source)
    grad_alignment = pullback(normed_grad)[0].astype(BF16)
    wo = wo.reshape(width // 4, chan, 4, width).transpose(3, 0, 2, 1).reshape(width * width, chan)
    weight_total = weight_total.T / total_res
    return (
        pair_update,
        grad_alignment,
        weight_total[:, :width],
        weight_total[:, width:],
        wo.astype(F32) / total_res,
    )


def solution(mesh):
    placed = (
        P(("groups", "seq"), "dap", None),
        P("groups", None),
        P(("groups", "dap"), None),
        P(("groups", "dap"), "seq", "chan"),
        P(),
        P(),
        P(None, "chan"),
    )
    return jax.shard_map(
        body,
        mesh=mesh,
        in_specs=placed,
        out_specs=(
            P(("groups", "dap"), "seq", "chan"),
            P(("groups", "seq"), "dap", None),
            P("groups", None),
            P("groups", None),
            P("groups", "chan"),
        ),
        check_vma=False,
    )
```

time: 344 us -> 60.6 us (0.18)
  local copies, waits for them, and re-layouts: 137 us -> 13.3 us
  waiting for transfers between devices: 81 us -> 0 us
  matrix products: 67.2 us -> 1.79 us
  Pallas kernels: 0 us -> 40 us
  blocking collectives: 26.7 us -> 0 us
  between operations: 15.6 us -> 0.95 us
  other arithmetic: 9.65 us -> 4.14 us
  starting transfers between devices: 3.84 us -> 0 us
    dot_general x28 -> x4, matrix products: 67.2 us -> 1.79 us  [dot(): lax.dot_general(a, b, (((ca,), (cb,)), ((), ())), preferred_element_type=...]
    psum x3 -> x0, waiting for transfers between devices: 61.1 us -> none  [the longest x2 61.1 us: body(): lax.psum((wo_part, left_wpart, right_wpart), ('dap', 'seq'))]
    convert_element_type x8 -> x0, local copies, waits for them, and re-layouts: 53.6 us -> none  [the longest x6 52 us: outer_block(): outer_prod = jnp.einsum('ksic,ksjd->kijcd', left_blocks, right_cols, pref...]
    pallas_call x0 -> x4, Pallas kernels: none -> 40 us  [the longest x1 16.9 us: body(): vmem_call(functools.partial(reduce_kernel, dap, seq), (shape((2, half, fl...]
    all_gather x3 -> x0, blocking collectives: 26.7 us -> none  [the longest x1 14.1 us: body(): lax.all_gather(right_act.reshape(seq_rows, res_rows * outer_width), 'dap'...]
    reduce_sum x3 -> x0, local copies, waits for them, and re-layouts: 26.3 us -> none  [weight_step(): jnp.einsum('kpf,pe->fe', outer_block(offset), own_cols, preferred_element...]
    dot_general x3 -> x0, local copies, waits for them, and re-layouts: 26.3 us -> none  [forward_step(): jnp.einsum('kpf,fe->pe', outer_block(offset), out_weight, preferred_eleme...]
    reduce_scatter x2 -> x0, waiting for transfers between devices: 19.8 us -> none  [the longest x1 19.8 us: body(): lax.psum_scatter(right_part.reshape(seq_rows, total_res * outer_width), '...]
  transfers between devices with their start and end apart: 6 -> 0, of which waited for: 2 -> 0; matrix products, arithmetic and copies ran while one was open for 47% -> 0% of each run, Pallas kernels for 0% -> 0%
where the time goes in v1:
time: 60.6 us; the launch traced here: 60.1 us
  Pallas kernels  40 us (66%)
  local copies, waits for them, and re-layouts  13.3 us (22%)
  other arithmetic  4.14 us (7%)
  matrix products  1.79 us (3%)
  between operations  0.95 us (2%)
    pallas_call x1, Pallas kernels, body(): vmem_call(functools.partial(reduce_kernel, dap, seq), (shape((2, half, fl...  16.9 us
    pallas_call x1, Pallas kernels, body(): vmem_call(functools.partial(gather_kernel, dap, seq), (shape((seq, seqs,...  10.3 us
    pallas_call x1, Pallas kernels, body(): vmem_call(functools.partial(total_kernel, dap, seq), shape((2 * width, ch...  7.11 us
    pallas_call x1, Pallas kernels, body(): vmem_call(main_kernel, (shape((rows, cols, chan), BF16), shape((all_seqs,...  5.72 us
    unnamed x17, local copies, waits for them, and re-layouts  3.17 us
    reshape x2, local copies, waits for them, and re-layouts, body(): right_t = right_t.reshape(all_seqs, width * cols)  2.89 us
    dot_general x4, matrix products, dot(): lax.dot_general(a, b, (((ca,), (cb,)), ((), ())), preferred_element_type=...  1.79 us
    reshape x1, local copies, waits for them, and re-layouts, body(): dr = drt.reshape(seq, 2, half, width, per, rows).transpose(1, 4, 0, 2, 5, 3)  1.69 us

profile of v1, /device:TPU:0, one launch (start us, length us, event | category | flops | bytes accessed | tf_op | source)
XLA Modules:
  0.0 60.1 jit_solution(8394752794623706151)
XLA Ops:
  0.7 0.8 %dynamic-slice_convert_fusion = f32[32,24]{1,0:T(8,128)S(1)} fusion(s32[64,96]{1,0:T(8,128)} %param.8, s32[]{:T(128)S(6)} %select_n.11, s32[]{:T(128)S(6)} %select_n.12), kind=kLoop, calls=%fused_computation.29 | loop fusion | flops 768 | bytes 6152 | tf_op jit(solution)/shard_map/convert_element_type | solution.py:365
  1.5 1.2 %convert_reduce_fusion = f32[32,24]{1,0:T(8,128)S(1)} fusion(bf16[32,24,256]{2,1,0:T(8,128)(2,1)} %param.7), kind=kLoop, calls=%fused_computation.7 | loop fusion | flops 392448 | bytes 396288 | tf_op jit(solution)/shard_map/reduce_sum | solution.py:17
  3.1 0.7 %copy-done.5 = bf16[256,32]{0,1:T(8,128)(2,1)S(1)} copy-done((bf16[256,32]{0,1:T(8,128)(2,1)S(1)}, bf16[256,32]{0,1:T(8,128)(2,1)}, u32[]{:S(2)}) %copy-start.5) | copy-done | bytes 16408
  3.8 0.4 fusion
  4.5 0.3 reshape.98.right_ref
  5.0 10.3 %shard_map.110 = (bf16[2,32,768]{2,1,0:T(8,128)(2,1)S(1)}, bf16[2,2,32,768]{3,2,1,0:T(8,128)(2,1)S(1)}) custom-call(bf16[32,768]{1,0:T(8,128)(2,1)S(1)} %reshape.97.left_ref, bf16[32,768]{1,0:T(8,128)(2,1)S(1)} %reshape.98.right_ref), custom_call_target="tpu_custom_call" | custom-call | tf_op jit(solution)/shard_map/pallas_call | solution.py:382
  15.3 1.7 %reshape.100 = bf16[2,2,32,32,24]{4,3,2,1,0:T(8,128)(2,1)S(1)} reshape(bf16[2,2,32,768]{3,2,1,0:T(8,128)(2,1)S(1)} %get-tuple-element.15) | data formatting | bytes 393216 | tf_op jit(solution)/shard_map/reshape | solution.py:394
  17.0 1.1 %copy.38 = bf16[2,32,32,2,24]{4,3,2,1,0:T(2,128)(2,1)S(1)} copy(bf16[2,32,32,2,24]{4,2,1,0,3:T(8,128)(2,1)S(1)} %bitcast.38) | data formatting | bytes 393216 | tf_op jit(solution)/shard_map/reshape | solution.py:395
  18.1 1.8 %reshape.109.rt_ref = bf16[64,1536]{1,0:T(8,128)(2,1)S(1)} reshape(bf16[2,32,32,2,24]{4,3,2,1,0:T(2,128)(2,1)S(1)} %copy.38) | data formatting | bytes 393216 | tf_op jit(solution)/shard_map/reshape | solution.py:395
  20.3 0.5 copy-done.3
  21.1 0.8 %copy-done.1 = bf16[24,48,64]{2,1,0:T(8,128)(2,1)S(1)} copy-done((bf16[24,48,64]{2,1,0:T(8,128)(2,1)S(1)}, bf16[24,48,64]{2,1,0:T(8,128)(2,1)}, u32[]{:S(2)}) %copy-start.1) | copy-done | bytes 147480
  21.9 5.7 %shard_map.111 = (bf16[24,48,64]{2,1,0:T(8,128)(2,1)}, bf16[64,768]{1,0:T(8,128)(2,1)S(1)}, bf16[64,1536]{1,0:T(8,128)(2,1)S(1)}, bf16[8,64,128]{2,1,0:T(8,128)(2,1)S(1)}) custom-call(bf16[64,768]{1,0:T(8,128)(2,1)S(1)} %bitcast.36, bf16[64,1536]{1,0:T(8,128)(2,1)S(1)} %reshape.109.rt_ref, bf16[1024,64]{1,0:T(8,128)(2,1)S(1)} %bitcast.33, ...), custom_call_target="tpu_custom_call" | custom-call | tf_op jit(solution)/shard_map/pallas_call | solution.py:399
  27.7 1.7 %reshape.105 = bf16[2,2,16,32,2,24]{5,4,3,2,1,0:T(2,128)(2,1)S(1)} reshape(bf16[64,1536]{1,0:T(8,128)(2,1)S(1)} %get-tuple-element.18) | data formatting | bytes 393216 | tf_op jit(solution)/shard_map/reshape | solution.py:417
  29.4 0.9 %copy.29 = bf16[2,2,2,16,24,32]{5,4,3,2,1,0:T(8,128)(2,1)S(1)} copy(bf16[2,2,2,16,24,32]{4,1,5,3,0,2:T(2,128)(2,1)S(1)} %bitcast.37) | data formatting | bytes 393216 | tf_op jit(solution)/shard_map/transpose | solution.py:417
  30.2 0.5 reshape.106.dr_ref
  30.7 16.9 %shard_map.112 = (bf16[2,16,768]{2,1,0:T(8,128)(2,1)S(1)}, bf16[2,16,768]{2,1,0:T(8,128)(2,1)S(1)}, bf16[8,64,128]{2,1,0:T(8,128)(2,1)S(1)}) custom-call(bf16[2,2,16,768]{3,2,1,0:T(8,128)(2,1)S(1)} %bitcast.34, bf16[2,2,2,16,768]{4,3,2,1,0:T(8,128)(2,1)S(1)} %reshape.106.dr_ref, bf16[8,64,128]{2,1,0:T(8,128)(2,1)S(1)} %get-tuple-element.19.wo_ref), custom_call_target="tpu_custom_call" | custom-call | tf_op jit(solution)/shard_map/pallas_call | solution.py:420
  48.0 0.6 %convolution_bitcast_fusion.part_ref = f32[64,256]{1,0:T(8,128)S(1)} fusion(bf16[32,24,256]{2,1,0:T(8,128)(2,1)S(1)} %copy-done.2, f32[32,24]{1,0:T(8,128)S(1)} %fusion.15, f32[32,24]{1,0:T(8,128)S(1)} %broadcast_multiply_fusion, bf16[32,24,32]{2,1,0:T(8,128)(2,1)S(1)} %concatenate.14, bf16[32,24,32]{2,1,0:T(8,128)(2,1)S(1)} %concatenate.13, ...), kind=kOutput, calls=%fused_computation.3 | convolution fusion | flops 26247168 | bytes 566272 | tf_op jit(solution)/shard_map/dot_general | solution.py:23
  48.6 7.1 %shard_map.113 = f32[64,256]{1,0:T(8,128)S(1)} custom-call(f32[64,256]{1,0:T(8,128)S(1)} %convolution_bitcast_fusion.part_ref), custom_call_target="tpu_custom_call" | custom-call | tf_op jit(solution)/shard_map/pallas_call | solution.py:451
  55.8 0.6 %fusion.19 = (f32[256,32]{0,1:T(8,128)}, f32[256,32]{0,1:T(8,128)}) fusion(f32[256,64]{0,1:T(8,128)S(1)} %multiply_bitcast_fusion), kind=kLoop, calls=%fused_computation.36 | loop fusion | bytes 131072 | tf_op jit(solution)/shard_map/slice | solution.py:471
  56.4 0.5 fusion.8
  56.9 0.5 fusion.9
  57.4 1.2 %add_convert_fusion = bf16[32,24,256]{2,1,0:T(8,128)(2,1)} fusion(f32[32,24]{1,0:T(8,128)S(1)} %negate_multiply_fusion, f32[32,24]{1,0:T(8,128)S(1)} %multiply_multiply_fusion, f32[32,24]{1,0:T(8,128)S(1)} %broadcast_multiply_fusion, bf16[32,24,256]{2,1,0:T(8,128)(2,1)S(1)} %copy-done.2, f32[32,24,256]{2,1,0:T(8,128)S(1)} %get-tuple-element.33, ...), kind=kLoop, calls=%fused_computation.15 | loop fusion | flops 1572864 | bytes 1585152 | tf_op jit(solution)/shard_map/convert_element_type | solution.py:464
  58.9 0.3 copy.33
  59.2 0.9 %copy.34 = f32[1024,64]{0,1:T(8,128)} copy(f32[1024,64]{1,0:T(8,128)S(1)} %bitcast.40) | data formatting | bytes 524288
  (31 shorter events, 2.1 us)
Async XLA Ops:
  0.6 19.3 %copy-start = (s32[24,96]{1,0:T(8,128)S(1)}, s32[24,96]{1,0:T(8,128)}, u32[]{:S(2)}) copy-start(s32[24,96]{1,0:T(8,128)} %param.9) | copy-start | bytes 27652
  0.6 2.1 %copy-start.2 = (bf16[32,24,256]{2,1,0:T(8,128)(2,1)S(1)}, bf16[32,24,256]{2,1,0:T(8,128)(2,1)}, u32[]{:S(2)}) copy-start(bf16[32,24,256]{2,1,0:T(8,128)(2,1)} %param.7) | copy-start | bytes 1179652
  3.0 0.7 %copy-start.5 = (bf16[256,32]{0,1:T(8,128)(2,1)S(1)}, bf16[256,32]{0,1:T(8,128)(2,1)}, u32[]{:S(2)}) copy-start(bf16[256,32]{0,1:T(8,128)(2,1)} %param.12) | copy-start | bytes 49156
  3.0 0.7 %copy-start.6 = (bf16[256,32]{0,1:T(8,128)(2,1)S(1)}, bf16[256,32]{0,1:T(8,128)(2,1)}, u32[]{:S(2)}) copy-start(bf16[256,32]{0,1:T(8,128)(2,1)} %param.11) | copy-start | bytes 49156
  18.1 2.0 %copy-start.4 = (s32[64,96]{1,0:T(8,128)S(1)}, s32[64,96]{1,0:T(8,128)}, u32[]{:S(2)}) copy-start(s32[64,96]{1,0:T(8,128)} %param.8) | copy-start | bytes 73732
  19.9 0.9 %copy-start.3 = (bf16[1024,64]{0,1:T(8,128)(2,1)S(1)}, bf16[1024,64]{0,1:T(8,128)(2,1)}, u32[]{:S(2)}) copy-start(bf16[1024,64]{0,1:T(8,128)(2,1)} %param.13) | copy-start | bytes 393220
  21.0 1.0 %copy-start.1 = (bf16[24,48,64]{2,1,0:T(8,128)(2,1)S(1)}, bf16[24,48,64]{2,1,0:T(8,128)(2,1)}, u32[]{:S(2)}) copy-start(bf16[24,48,64]{2,1,0:T(8,128)(2,1)} %cot_ref.1) | copy-start | bytes 442372

commit v2 on v1

v2 whole, which is shorter than its diff:
```python
import functools

import jax
import jax.numpy as jnp
from jax import lax
from jax.experimental import pallas as pl
from jax.experimental.pallas import tpu as pltpu
from jax.sharding import PartitionSpec as P

MESH = pl.DeviceIdType.MESH
VMEM_BYTES = 48 * 1024 * 1024
F32 = jnp.float32
BF16 = jnp.bfloat16


def layer_norm(values):
    center = values - jnp.mean(values, axis=-1, keepdims=True)
    variance = jnp.mean(center * center, axis=-1, keepdims=True)
    return center * lax.rsqrt(variance + 1e-05)


def dot(a, b, ca, cb):
    return lax.dot_general(a, b, (((ca,), (cb,)), ((), ())), preferred_element_type=F32)


def vmem_call(kernel, out_shape, scratch, num_in, collective_id=None):
    params = dict(vmem_limit_bytes=VMEM_BYTES)
    if collective_id is not None:
        params.update(collective_id=collective_id, has_side_effects=True)
    return pl.pallas_call(
        kernel,
        out_shape=out_shape,
        in_specs=[pl.BlockSpec(memory_space=pltpu.VMEM)] * num_in,
        out_specs=jax.tree.map(lambda _: pl.BlockSpec(memory_space=pltpu.VMEM), out_shape),
        scratch_shapes=scratch,
        compiler_params=pltpu.CompilerParams(**params),
    )


def plane_barrier(dap, seq):
    num = dap * seq
    me = lax.axis_index("dap") * seq + lax.axis_index("seq")
    barrier = pltpu.get_barrier_semaphore()
    for step in range(1, num):
        peer = lax.rem(me + step, num)
        pl.semaphore_signal(
            barrier,
            inc=1,
            device_id={"dap": peer // seq, "seq": lax.rem(peer, seq)},
            device_id_type=MESH,
        )
    return barrier, num - 1


def arrived(buf, sem):
    pltpu.make_async_copy(buf, buf, sem).wait()


def pair_kernel(
    dap, seq, left_ref, right_ref, w_ref, cot_ref, sct_ref, pu_ref, lg_ref, rg_ref, wo_ref,
    sg, wbd, outer, dout, lall, rt, lbuf, rbuf, dl, dr, dw,
    l1, r1, l2, r2, lin, rin, pair, wrecv,
    glsend, glrecv, grsend, grrecv, csend, crecv, lsend, lrecv, rsend, rrecv, wsend, wrsem,
):
    rows, cols, chan = cot_ref.shape
    seqs, flat = left_ref.shape
    width = flat // rows
    pack = 128 // width
    groups = rows // pack
    half = seqs // 2
    per = dap // seq
    num = dap * seq
    a = lax.axis_index("dap")
    q = lax.axis_index("seq")
    h = lax.axis_index("chan")
    other = 1 - h
    me = a * seq + q
    barrier, count = plane_barrier(dap, seq)
    pl.semaphore_signal(barrier, inc=1, device_id={"chan": other}, device_id_type=MESH)
    pl.semaphore_wait(barrier, count + 1)

    def plane_copy(src, dst, send, recv, peer_a, peer_q):
        return pltpu.make_async_remote_copy(
            src_ref=src, dst_ref=dst, send_sem=send, recv_sem=recv,
            device_id={"dap": peer_a, "seq": peer_q}, device_id_type=MESH,
        )

    def core_copy(src, dst, sem):
        return pltpu.make_async_remote_copy(
            src_ref=src, dst_ref=dst, send_sem=csend.at[sem], recv_sem=crecv.at[sem],
            device_id={"chan": other}, device_id_type=MESH,
        )

    def right_copy(step):
        return plane_copy(
            right_ref, rbuf.at[lax.rem(a, per), q], grsend.at[step],
            grrecv.at[lax.rem(a, per), q], lax.rem(a + step, dap), a // per,
        )

    def left_copy(step):
        return plane_copy(
            left_ref, lbuf.at[q], glsend.at[step], glrecv.at[q], a, lax.rem(q + step, seq)
        )

    own = a // per == q
    for step in range(1, dap):
        right_copy(step).start()
    pl.when(jnp.logical_not(own))(lambda: right_copy(0).start())
    for step in range(1, seq):
        left_copy(step).start()

    for g in range(groups):
        parts = [
            cot_ref[g * pack + k].astype(F32) * sct_ref[:, g * pack + k : g * pack + k + 1]
            for k in range(pack)
        ]
        sg[g * cols : (g + 1) * cols, :] = jnp.concatenate(parts, axis=1).astype(BF16)
    row_part = lax.broadcasted_iota(jnp.int32, (128, pack * chan), 0) // width
    lane_part = lax.broadcasted_iota(jnp.int32, (128, pack * chan), 1) // chan
    diagonal = (row_part == lane_part).astype(F32).astype(BF16)
    for d in range(width):
        block = w_ref[d * width : (d + 1) * width, :]
        block = jnp.concatenate([block] * pack, axis=1)
        wbd[d * 128 : (d + 1) * 128, :] = jnp.concatenate([block] * pack, axis=0) * diagonal
    for ch in range(width // 8):
        piece = dot(sg[...], wbd[ch * 1024 : (ch + 1) * 1024, :], 1, 1)
        for dd in range(0, 8, 2):
            for block in range(per):
                at = (block * width + ch * 8 + dd) * rows
                for g in range(groups):
                    start = g * cols + block * rows
                    dout[at : at + 2 * rows, g * 128 : (g + 1) * 128] = jnp.concatenate(
                        [
                            piece[start : start + rows, e * 128 : (e + 1) * 128]
                            for e in (dd, dd + 1)
                        ],
                        axis=0,
                    ).astype(BF16)

    for src_q in range(seq):
        at = src_q * seqs

        @pl.when(src_q != q)
        def _():
            arrived(lbuf.at[src_q], glrecv.at[src_q])
            lall[at : at + seqs, :] = lbuf[src_q]

        @pl.when(src_q == q)
        def _():
            lall[at : at + seqs, :] = left_ref[...]

        for block in range(per):
            mine = jnp.logical_and(q * per + block == a, src_q == q)

            @pl.when(jnp.logical_not(mine))
            def _():
                arrived(rbuf.at[block, src_q], grrecv.at[block, src_q])
                rt[at : at + seqs, block * flat : (block + 1) * flat] = rbuf[block, src_q]

            @pl.when(mine)
            def _():
                rt[at : at + seqs, block * flat : (block + 1) * flat] = right_ref[...]

    right_part = dot(lall[...], dout[...], 1, 1).astype(BF16)
    for dest_q in range(seq):
        for core in range(2):
            at = dest_q * seqs + core * half
            for block in range(per):
                dr[core, block, dest_q] = right_part[
                    at : at + half, block * flat : (block + 1) * flat
                ]
    right_core = core_copy(dr.at[other], r1, 1)
    right_core.start()
    left_part = dot(rt[...], dout[...], 1, 0).astype(BF16)
    for dest_q in range(seq):
        for core in range(2):
            at = dest_q * seqs + core * half
            dl[core, dest_q] = left_part[at : at + half, :]
    left_core = core_copy(dl.at[other], l1, 0)
    left_core.start()

    for ch in range(width // 16):
        pieces = []
        for block in range(per):
            at = (block * width + ch * 16) * rows
            pieces.append(dot(rt[:, at : at + 16 * rows], lall[...], 0, 0))
        for dd in range(16):
            at = (ch * 16 + dd) * 128
            for g in range(groups):
                outer[g * cols : (g + 1) * cols, at : at + 128] = jnp.concatenate(
                    [
                        piece[dd * rows : (dd + 1) * rows, g * 128 : (g + 1) * 128]
                        for piece in pieces
                    ],
                    axis=0,
                ).astype(BF16)

    def left_out(dest_q):
        return plane_copy(l2.at[dest_q], lin.at[q], lsend.at[dest_q], lrecv.at[q], a, dest_q)

    def right_out(block, dest_q):
        return plane_copy(
            r2.at[block, dest_q], rin.at[a], rsend.at[block, dest_q], rrecv.at[a],
            q * per + block, dest_q,
        )

    def is_me(block, dest_q):
        return jnp.logical_and(q * per + block == a, dest_q == q)

    right_core.wait()
    for block in range(per):
        for dest_q in range(seq):
            r2[block, dest_q] = (
                dr[h, block, dest_q].astype(F32) + r1[block, dest_q].astype(F32)
            ).astype(BF16)

            @pl.when(jnp.logical_not(is_me(block, dest_q)))
            def _():
                right_out(block, dest_q).start()

    left_core.wait()
    for dest_q in range(seq):
        l2[dest_q] = (dl[h, dest_q].astype(F32) + l1[dest_q].astype(F32)).astype(BF16)

        @pl.when(dest_q != q)
        def _():
            left_out(dest_q).start()

    lane_of = lax.broadcasted_iota(jnp.int32, (chan, 128), 1) // width
    wrows = dw.shape[1]
    for ch in range(width // pack):
        wide = dot(sg[...], outer[:, ch * pack * 128 : (ch + 1) * pack * 128], 0, 0)
        total = jnp.zeros((chan, 128), F32)
        for d in range(pack):
            part = jnp.zeros((chan, 128), F32)
            for k in range(pack):
                part = jnp.where(
                    lane_of == k,
                    wide[k * chan : (k + 1) * chan, d * 128 : (d + 1) * 128],
                    part,
                )
            part = part + pltpu.roll(part, 64, 1)
            part = part + pltpu.roll(part, 32, 1)
            total = jnp.where(lane_of == d, part, total)
        pieces = chan // wrows
        for p in range(pieces):
            dw[ch * pieces + p] = total[p * wrows : (p + 1) * wrows].astype(BF16)

    def scatter(step):
        peer = lax.rem(me + step, num)
        return plane_copy(
            dw.at[peer], wrecv.at[step], wsend.at[step], wrsem.at[step],
            peer // seq, lax.rem(peer, seq),
        )

    for step in range(1, num):
        scatter(step).start()

    projected = dot(outer[...], wbd[...], 1, 0)
    for g in range(groups):
        for k in range(pack):
            i = g * pack + k
            pu_ref[i] = (
                projected[g * cols : (g + 1) * cols, k * chan : (k + 1) * chan]
                * sct_ref[:, i : i + 1]
            ).astype(BF16)

    left_sum = l2[q].astype(F32)
    for step in range(1, seq):
        src_q = lax.rem(q + step, seq)
        arrived(lin.at[src_q], lrecv.at[src_q])
        left_sum = left_sum + lin[src_q].astype(F32)
    pair[h, 0] = left_sum.astype(BF16)

    @pl.when(own)
    def _():
        rin[a] = r2[lax.rem(a, per), q]

    @pl.when(jnp.logical_not(own))
    def _():
        arrived(rin.at[a], rrecv.at[a])

    right_sum = rin[a].astype(F32)
    for step in range(1, dap):
        src_a = lax.rem(a + step, dap)
        arrived(rin.at[src_a], rrecv.at[src_a])
        right_sum = right_sum + rin[src_a].astype(F32)
    pair[h, 1] = right_sum.astype(BF16)
    final = core_copy(pair.at[h], pair.at[h], 2)
    final.start()

    wo_sum = dw[me].astype(F32)
    for step in range(1, num):
        arrived(wrecv.at[step], wrsem.at[step])
        wo_sum = wo_sum + wrecv[step].astype(F32)
    wo_ref[...] = wo_sum.astype(BF16)

    final.wait_send()
    arrived(pair.at[other], crecv.at[2])
    for core in range(2):
        lg_ref[core * half : (core + 1) * half, :] = pair[core, 0]
        rg_ref[core * half : (core + 1) * half, :] = pair[core, 1]

    for step in range(1, dap):
        right_copy(step).wait_send()
    pl.when(jnp.logical_not(own))(lambda: right_copy(0).wait_send())
    for step in range(1, seq):
        left_copy(step).wait_send()
    for step in range(1, num):
        scatter(step).wait_send()
    for dest_q in range(seq):

        @pl.when(dest_q != q)
        def _():
            left_out(dest_q).wait_send()

        for block in range(per):

            @pl.when(jnp.logical_not(is_me(block, dest_q)))
            def _():
                right_out(block, dest_q).wait_send()


def finish_kernel(
    dap, seq, total_res, grads_ref, normed_ref, source_ref, weight_ref, wo_ref,
    ga_ref, wl_ref, wr_ref, wog_ref,
    part, inbox, sums, wall, send, recv, gsend, grecv, csend, crecv,
):
    num = dap * seq
    width = wl_ref.shape[1]
    chan = wog_ref.shape[1]
    pack = 128 // width
    h = lax.axis_index("chan")
    other = 1 - h
    me = lax.axis_index("dap") * seq + lax.axis_index("seq")
    barrier, count = plane_barrier(dap, seq)
    pl.semaphore_signal(barrier, inc=1, device_id={"chan": other}, device_id_type=MESH)
    products = dot(grads_ref[...], normed_ref[...], 0, 0).astype(BF16)
    for core in range(2):
        part[core] = products[core * width : (core + 1) * width]
    wall[me] = wo_ref[...]
    pl.semaphore_wait(barrier, count + 1)

    def plane_copy(src, dst, send_sem, recv_sem, step):
        peer = lax.rem(me + step, num)
        return pltpu.make_async_remote_copy(
            src_ref=src, dst_ref=dst, send_sem=send_sem, recv_sem=recv_sem,
            device_id={"dap": peer // seq, "seq": lax.rem(peer, seq)}, device_id_type=MESH,
        )

    def part_copy(step):
        return plane_copy(part.at[h], inbox.at[step], send.at[step], recv.at[step], step)

    def wo_copy(step):
        return plane_copy(wall.at[me], wall.at[me], gsend.at[step], grecv.at[me], step)

    for step in range(1, num):
        part_copy(step).start()
    for step in range(1, num):
        wo_copy(step).start()

    values = source_ref[...].astype(F32)
    center = values - jnp.mean(values, axis=-1, keepdims=True)
    spread = lax.rsqrt(jnp.mean(center * center, axis=-1, keepdims=True) + 1e-05)
    normal = center * spread
    grad = dot(grads_ref[...], weight_ref[...], 1, 1)
    along = jnp.mean(grad * normal, axis=-1, keepdims=True)
    level = jnp.mean(grad, axis=-1, keepdims=True)
    ga_ref[...] = (spread * (grad - level - normal * along)).astype(BF16)

    inbox[0] = part[h]
    for step in range(1, num):
        part_copy(step).wait()
    total = jnp.zeros(sums.shape[1:], F32)
    for source in range(num):
        total = total + inbox[lax.rem(me - source + num, num)].astype(F32)
    sums[h] = total / total_res
    exchange = pltpu.make_async_remote_copy(
        src_ref=sums.at[h], dst_ref=sums.at[h], send_sem=csend, recv_sem=crecv,
        device_id={"chan": other}, device_id_type=MESH,
    )
    exchange.start()
    for step in range(1, num):
        src = lax.rem(me + step, num)
        arrived(wall.at[src], grecv.at[src])
    pieces = num * pack // width
    for ch in range(width // pack):
        tall = jnp.concatenate(
            [wall[ch * pieces + p].astype(F32) for p in range(pieces)], axis=0
        ).T / total_res
        for d in range(pack):
            wog_ref[pl.ds(ch * pack + d, width, stride=width), :] = tall[
                d * width : (d + 1) * width, :
            ]
    exchange.wait_send()
    arrived(sums.at[other], crecv)
    wl_ref[...] = sums[0].T
    wr_ref[...] = sums[1].T
    for step in range(1, num):
        wo_copy(step).wait_send()


def body(alignment, align_mask, pair_mask, cotangent, left_weight, right_weight, out_weight):
    seqs, rows, chans = alignment.shape
    width = left_weight.shape[1]
    chan = out_weight.shape[1]
    dap, seq = lax.axis_size("dap"), lax.axis_size("seq")
    per, num = dap // seq, dap * seq
    total_res, all_seqs = rows * dap, seqs * seq
    cols = total_res // seq
    a, q = lax.axis_index("dap"), lax.axis_index("seq")
    half = seqs // 2
    flat = rows * width

    mask_bf = align_mask.astype(BF16)
    own_mask = lax.dynamic_slice(align_mask, (q * seqs, a * rows), (seqs, rows)).astype(F32)
    mask_rows = lax.dynamic_slice_in_dim(mask_bf, a * rows, rows, 1)
    mask_cols = lax.dynamic_slice_in_dim(mask_bf, q * cols, cols, 1)
    counts = dot(mask_cols, mask_rows, 0, 0)
    own_pairs = lax.dynamic_slice_in_dim(pair_mask, q * cols, cols, 1)
    scale_t = own_pairs.T.astype(F32) / (counts + 0.001)

    normed = layer_norm(alignment.astype(F32)).astype(BF16).reshape(seqs * rows, chans)
    both_weights = jnp.concatenate([left_weight, right_weight], axis=1)
    act = dot(normed, both_weights, 1, 0)
    act = (own_mask[:, :, None] * act.reshape(seqs, rows, 2 * width)).astype(BF16)
    left = act[:, :, :width].reshape(seqs, flat)
    right = act[:, :, width:].transpose(0, 2, 1).reshape(seqs, flat)
    w_dc = out_weight.reshape(width, width, chan).transpose(1, 0, 2).reshape(width * width, chan)

    dma = pltpu.SemaphoreType.DMA
    shape = jax.ShapeDtypeStruct
    groups = rows // 4
    wrows = width // 4 * chan // num

    def room(*dims):
        return pltpu.VMEM(dims, BF16)

    pair_update, lg, rg, wo = vmem_call(
        functools.partial(pair_kernel, dap, seq),
        (
            shape((rows, cols, chan), BF16),
            shape((seqs, flat), BF16),
            shape((seqs, flat), BF16),
            shape((wrows, 128), BF16),
        ),
        [
            room(groups * cols, 4 * chan),
            room(width * 128, 4 * chan),
            room(groups * cols, width * 128),
            room(width * cols, groups * 128),
            room(all_seqs, flat),
            room(all_seqs, width * cols),
            room(seq, seqs, flat),
            room(per, seq, seqs, flat),
            room(2, seq, half, flat),
            room(2, per, seq, half, flat),
            room(num, wrows, 128),
            room(seq, half, flat),
            room(per, seq, half, flat),
            room(seq, half, flat),
            room(per, seq, half, flat),
            room(seq, half, flat),
            room(dap, half, flat),
            room(2, 2, half, flat),
            room(num, wrows, 128),
            dma((seq,)), dma((seq,)), dma((dap,)), dma((per, seq)),
            dma((3,)), dma((3,)),
            dma((seq,)), dma((seq,)),
            dma((per, seq)), dma((dap,)),
            dma((num,)), dma((num,)),
        ],
        5,
        0,
    )(left, right, w_dc, cotangent, scale_t)

    grads = jnp.concatenate(
        [lg.reshape(seqs, rows, width), rg.reshape(seqs, width, rows).transpose(0, 2, 1)], axis=2
    )
    grads = (grads.astype(F32) * own_mask[:, :, None]).astype(BF16).reshape(seqs * rows, 2 * width)
    grad_alignment, wl, wr, wog = vmem_call(
        functools.partial(finish_kernel, dap, seq, total_res),
        (
            shape((seqs * rows, chans), BF16),
            shape((chans, width), F32),
            shape((chans, width), F32),
            shape((width * width, chan), F32),
        ),
        [
            room(2, width, chans),
            room(num, width, chans),
            pltpu.VMEM((2, width, chans), F32),
            room(num, wrows, 128),
            dma((num,)), dma((num,)), dma((num,)), dma((num,)), dma, dma,
        ],
        5,
        1,
    )(grads, normed, alignment.reshape(seqs * rows, chans), both_weights, wo)
    return pair_update, grad_alignment.reshape(seqs, rows, chans), wl, wr, wog


def solution(mesh):
    placed = (
        P(("groups", "seq"), "dap", None),
        P("groups", None),
        P(("groups", "dap"), None),
        P(("groups", "dap"), "seq", "chan"),
        P(),
        P(),
        P(None, "chan"),
    )
    return jax.shard_map(
        body,
        mesh=mesh,
        in_specs=placed,
        out_specs=(
            P(("groups", "dap"), "seq", "chan"),
            P(("groups", "seq"), "dap", None),
            P("groups", None),
            P("groups", None),
            P("groups", "chan"),
        ),
        check_vma=False,
    )
```

time: 60.6 us -> 48.1 us (0.79)
  Pallas kernels: 40 us -> 33.5 us
  local copies, waits for them, and re-layouts: 13.3 us -> 9.07 us
  matrix products: 1.79 us -> 0.54 us
    pallas_call x4 -> x2, Pallas kernels: 40 us -> 33.5 us  [the longest x1 22.2 us: body(): vmem_call(functools.partial(pair_kernel, dap, seq), (shape((rows, cols, c...]
    reshape x6 -> x1, local copies, waits for them, and re-layouts: 6.75 us -> 0.38 us  [body(): rg.reshape(seqs, width, rows).transpose(0, 2, 1)]
    unnamed x17 -> x21, local copies, waits for them, and re-layouts: 3.17 us -> 7.33 us
    dot_general x4 -> x2, matrix products: 1.79 us -> 0.54 us  [dot(): lax.dot_general(a, b, (((ca,), (cb,)), ((), ())), preferred_element_type=...]
    convert_element_type x1, other arithmetic: 0.01 us -> 0.76 us  [body(): mask_bf = align_mask.astype(BF16)]
    convert_element_type x1 -> x2, other arithmetic: 1.23 us -> 0.49 us  [the longest x1 0.27 us: body(): layer_norm(alignment.astype(F32)).astype(BF16).reshape(seqs * rows, chans)]
    transpose x1, local copies, waits for them, and re-layouts: 0.86 us -> 0.16 us  [body(): rg.reshape(seqs, width, rows).transpose(0, 2, 1)]
    slice x1 -> x0, local copies, waits for them, and re-layouts: 0.63 us -> none  [body(): weight_total[:, width:]]
where the time goes in v2:
time: 48.1 us; the launch traced here: 47.6 us
  Pallas kernels  33.5 us (70%)
  local copies, waits for them, and re-layouts  9.07 us (19%)
  other arithmetic  3.64 us (8%)
  between operations  0.83 us (2%)
  matrix products  0.54 us (1%)
    pallas_call x1, Pallas kernels, body(): vmem_call(functools.partial(pair_kernel, dap, seq), (shape((rows, cols, c...  22.2 us
    pallas_call x1, Pallas kernels, body(): vmem_call(functools.partial(finish_kernel, dap, seq, total_res), (shape((...  11.3 us
    unnamed x21, local copies, waits for them, and re-layouts  7.33 us
    reduce_sum x1, other arithmetic, layer_norm(): center = values - jnp.mean(values, axis=-1, keepdims=True)  1.17 us

profile of v2, /device:TPU:0, one launch (start us, length us, event | category | flops | bytes accessed | tf_op | source)
XLA Modules:
  0.0 47.6 jit_solution(12763480814382228128)
XLA Ops:
  0.7 0.7 %copy-done = s32[24,96]{1,0:T(8,128)S(1)} copy-done((s32[24,96]{1,0:T(8,128)S(1)}, s32[24,96]{1,0:T(8,128)}, u32[]{:S(2)}) %copy-start) | copy-done | bytes 9240
  1.5 0.8 %dynamic-slice_convert_fusion = f32[32,24]{1,0:T(8,128)S(1)} fusion(s32[64,96]{1,0:T(8,128)} %param.8, s32[]{:T(128)S(6)} %select_n.11, s32[]{:T(128)S(6)} %select_n.12), kind=kLoop, calls=%fused_computation.17 | loop fusion | flops 768 | bytes 6152 | tf_op jit(solution)/shard_map/convert_element_type | solution.py:416
  2.4 0.8 %convert_element_type.35 = bf16[64,96]{1,0:T(8,128)(2,1)S(1)} convert(s32[64,96]{1,0:T(8,128)} %param.8) | non-fusion elementwise | flops 6144 | bytes 36864 | tf_op jit(solution)/shard_map/convert_element_type | solution.py:415
  3.1 0.3 fusion.1.sct_ref
  3.4 1.2 %convert_reduce_fusion = f32[32,24]{1,0:T(8,128)S(1)} fusion(bf16[32,24,256]{2,1,0:T(8,128)(2,1)} %param.7), kind=kLoop, calls=%fused_computation.5 | loop fusion | flops 392448 | bytes 396288 | tf_op jit(solution)/shard_map/reduce_sum | solution.py:17
  4.6 0.3 fusion.4
  5.0 0.7 %copy-done.4 = bf16[256,32]{0,1:T(8,128)(2,1)S(1)} copy-done((bf16[256,32]{0,1:T(8,128)(2,1)S(1)}, bf16[256,32]{0,1:T(8,128)(2,1)}, u32[]{:S(2)}) %copy-start.4) | copy-done | bytes 16408
  5.8 0.6 %copy-done.5 = bf16[256,32]{0,1:T(8,128)(2,1)S(1)} copy-done((bf16[256,32]{0,1:T(8,128)(2,1)S(1)}, bf16[256,32]{0,1:T(8,128)(2,1)}, u32[]{:S(2)}) %copy-start.5) | copy-done | bytes 16408
  6.6 0.7 %copy-done.3 = bf16[1024,64]{0,1:T(8,128)(2,1)S(1)} copy-done((bf16[1024,64]{0,1:T(8,128)(2,1)S(1)}, bf16[1024,64]{0,1:T(8,128)(2,1)}, u32[]{:S(2)}) %copy-start.3) | copy-done | bytes 131096
  7.6 0.3 fusion.5
  7.8 0.3 fusion
  8.4 0.2 copy.24
  8.6 0.3 reshape.57.right_ref
  8.9 0.5 copy-done.2
  9.4 22.2 %shard_map.110 = (bf16[24,48,64]{2,1,0:T(8,128)(2,1)S(1)}, bf16[32,768]{1,0:T(8,128)(2,1)S(1)}, bf16[32,768]{1,0:T(8,128)(2,1)S(1)}, bf16[64,128]{1,0:T(8,128)(2,1)S(1)}) custom-call(bf16[32,768]{1,0:T(8,128)(2,1)S(1)} %reshape.56.left_ref, bf16[32,768]{1,0:T(8,128)(2,1)S(1)} %reshape.57.right_ref, bf16[1024,64]{1,0:T(8,128)(2,1)S(1)} %bitcast.19, ...), custom_call_target="tpu_custom_call" | custom-call | tf_op jit(solution)/shard_map/pallas_call | solution.py:439
  31.6 0.2 concatenate.12
  31.8 0.4 reshape.60
  32.4 0.2 multiply_convert_fusion.grads_ref
  32.6 11.3 %shard_map.111 = (bf16[768,256]{1,0:T(8,128)(2,1)S(1)}, f32[256,32]{1,0:T(8,128)S(1)}, f32[256,32]{1,0:T(8,128)S(1)}, f32[1024,64]{1,0:T(8,128)S(1)}) custom-call(bf16[768,64]{1,0:T(8,128)(2,1)S(1)} %multiply_convert_fusion.grads_ref, bf16[768,256]{1,0:T(8,128)(2,1)S(1)} %bitcast.18, bf16[768,256]{1,0:T(8,128)(2,1)S(1)} %bitcast.17, ...), custom_call_target="tpu_custom_call" | custom-call | tf_op jit(solution)/shard_map/pallas_call | solution.py:481
  43.9 0.7 %copy.30 = f32[256,32]{0,1:T(8,128)} copy(f32[256,32]{1,0:T(8,128)S(1)} %get-tuple-element.28) | data formatting | bytes 65536
  44.6 0.7 %copy.31 = f32[256,32]{0,1:T(8,128)} copy(f32[256,32]{1,0:T(8,128)S(1)} %get-tuple-element.29) | data formatting | bytes 65536
  45.3 0.9 %copy.32 = f32[1024,64]{0,1:T(8,128)} copy(f32[1024,64]{1,0:T(8,128)S(1)} %get-tuple-element.30) | data formatting | bytes 524288
  46.2 0.7 %copy.37 = bf16[24,48,64]{2,1,0:T(8,128)(2,1)} copy(bf16[24,48,64]{2,1,0:T(8,128)(2,1)S(1)} %get-tuple-element.38) | data formatting | bytes 294912
  46.9 0.7 %copy.38 = bf16[32,24,256]{2,1,0:T(8,128)(2,1)} copy(bf16[32,24,256]{2,1,0:T(8,128)(2,1)S(1)} %bitcast.20) | data formatting | bytes 786432
  (20 shorter events, 1.3 us)
Async XLA Ops:
  0.6 0.7 %copy-start = (s32[24,96]{1,0:T(8,128)S(1)}, s32[24,96]{1,0:T(8,128)}, u32[]{:S(2)}) copy-start(s32[24,96]{1,0:T(8,128)} %param.9) | copy-start | bytes 27652
  0.6 4.0 %copy-start.1 = (bf16[32,24,256]{2,1,0:T(8,128)(2,1)S(1)}, bf16[32,24,256]{2,1,0:T(8,128)(2,1)}, u32[]{:S(2)}) copy-start(bf16[32,24,256]{2,1,0:T(8,128)(2,1)} %param.7) | copy-start | bytes 1179652
  4.9 0.7 %copy-start.4 = (bf16[256,32]{0,1:T(8,128)(2,1)S(1)}, bf16[256,32]{0,1:T(8,128)(2,1)}, u32[]{:S(2)}) copy-start(bf16[256,32]{0,1:T(8,128)(2,1)} %param.11) | copy-start | bytes 49156
  5.6 0.7 %copy-start.5 = (bf16[256,32]{0,1:T(8,128)(2,1)S(1)}, bf16[256,32]{0,1:T(8,128)(2,1)}, u32[]{:S(2)}) copy-start(bf16[256,32]{0,1:T(8,128)(2,1)} %param.12) | copy-start | bytes 49156
  6.4 0.9 %copy-start.3 = (bf16[1024,64]{0,1:T(8,128)(2,1)S(1)}, bf16[1024,64]{0,1:T(8,128)(2,1)}, u32[]{:S(2)}) copy-start(bf16[1024,64]{0,1:T(8,128)(2,1)} %param.13) | copy-start | bytes 393220
  8.4 1.0 %copy-start.2 = (bf16[24,48,64]{2,1,0:T(8,128)(2,1)S(1)}, bf16[24,48,64]{2,1,0:T(8,128)(2,1)}, u32[]{:S(2)}) copy-start(bf16[24,48,64]{2,1,0:T(8,128)(2,1)} %cot_ref.1) | copy-start | bytes 442372

commit v3 on v2

--- a/solution.py
+++ b/solution.py
@@ -8,33 +8,13 @@
 from jax.sharding import PartitionSpec as P
 
 MESH = pl.DeviceIdType.MESH
-VMEM_BYTES = 48 * 1024 * 1024
+VMEM_BYTES = 62 * 1024 * 1024
 F32 = jnp.float32
 BF16 = jnp.bfloat16
 
 
-def layer_norm(values):
-    center = values - jnp.mean(values, axis=-1, keepdims=True)
-    variance = jnp.mean(center * center, axis=-1, keepdims=True)
-    return center * lax.rsqrt(variance + 1e-05)
-
-
 def dot(a, b, ca, cb):
     return lax.dot_general(a, b, (((ca,), (cb,)), ((), ())), preferred_element_type=F32)
-
-
-def vmem_call(kernel, out_shape, scratch, num_in, collective_id=None):
-    params = dict(vmem_limit_bytes=VMEM_BYTES)
-    if collective_id is not None:
-        params.update(collective_id=collective_id, has_side_effects=True)
-    return pl.pallas_call(
-        kernel,
-        out_shape=out_shape,
-        in_specs=[pl.BlockSpec(memory_space=pltpu.VMEM)] * num_in,
-        out_specs=jax.tree.map(lambda _: pl.BlockSpec(memory_space=pltpu.VMEM), out_shape),
-        scratch_shapes=scratch,
-        compiler_params=pltpu.CompilerParams(**params),
-    )
 
 
 def plane_barrier(dap, seq):
@@ -56,15 +36,22 @@
     pltpu.make_async_copy(buf, buf, sem).wait()
 
 
-def pair_kernel(
-    dap, seq, left_ref, right_ref, w_ref, cot_ref, sct_ref, pu_ref, lg_ref, rg_ref, wo_ref,
+def whole_kernel(
+    dap, seq, total_res,
+    align_hbm, amask_hbm, pmask_hbm, cot_hbm, lw_hbm, rw_hbm, ow_hbm,
+    pu_ref, ga_ref, wl_ref, wr_ref, wog_ref,
+    align_ref, amask, pmask, cot_ref, lw_ref, rw_ref, ow_ref,
+    normal, normed, spreads, act, mask_rows, w_cd, perm, left_ref, right_ref, wtall,
     sg, wbd, outer, dout, lall, rt, lbuf, rbuf, dl, dr, dw,
     l1, r1, l2, r2, lin, rin, pair, wrecv,
-    glsend, glrecv, grsend, grrecv, csend, crecv, lsend, lrecv, rsend, rrecv, wsend, wrsem,
+    wpart, inbox, sums, wall,
+    load, glsend, glrecv, grsend, grrecv, csend, crecv, lsend, lrecv, rsend, rrecv, wsend, wrsem,
+    psend, precv, asend, arecv,
 ):
     rows, cols, chan = cot_ref.shape
     seqs, flat = left_ref.shape
     width = flat // rows
+    chans = align_ref.shape[2]
     pack = 128 // width
     groups = rows // pack
     half = seqs // 2
@@ -77,6 +64,57 @@
     me = a * seq + q
     barrier, count = plane_barrier(dap, seq)
     pl.semaphore_signal(barrier, inc=1, device_id={"chan": other}, device_id_type=MESH)
+    loads = [
+        pltpu.make_async_copy(src, dst, load.at[n])
+        for n, (src, dst) in enumerate(
+            [
+                (align_hbm, align_ref), (lw_hbm, lw_ref), (rw_hbm, rw_ref), (amask_hbm, amask),
+                (pmask_hbm, pmask), (cot_hbm, cot_ref), (ow_hbm, ow_ref),
+            ]
+        )
+    ]
+    for copy in loads:
+        copy.start()
+
+    column = lax.broadcasted_iota(jnp.int32, (1, flat), 1)
+    d_of = (column * ((65536 + rows - 1) // rows)) >> 16
+    source_of = (column - d_of * rows) * width + d_of
+    perm[...] = jnp.where(
+        lax.broadcasted_iota(jnp.int32, (flat, flat), 0) == source_of, 1.0, 0.0
+    ).astype(BF16)
+
+    for copy in loads[:4]:
+        copy.wait()
+    values = align_ref[...].astype(F32).reshape(seqs * rows, chans)
+    center = values - jnp.mean(values, axis=-1, keepdims=True)
+    spread = lax.rsqrt(jnp.mean(center * center, axis=-1, keepdims=True) + 1e-05)
+    spreads[...] = spread
+    normal[...] = center * spread
+    normed[...] = normal[...].astype(BF16)
+    both = jnp.concatenate([lw_ref[...], rw_ref[...]], axis=0)
+    act[...] = dot(normed[...], both, 1, 1).reshape(seqs, rows, 2 * width)
+
+    def pick(size, start):
+        shape = (total_res, size)
+        row = lax.broadcasted_iota(jnp.int32, shape, 0)
+        lane = lax.broadcasted_iota(jnp.int32, shape, 1)
+        return jnp.where(row == lane + start, 1.0, 0.0).astype(BF16)
+
+    mask_all = amask[...].astype(F32).astype(BF16)
+    row_pick = pick(rows, a * rows)
+    col_pick = pick(cols, q * cols)
+    mask_rows[...] = dot(mask_all, row_pick, 1, 0)
+    own_mask = mask_rows[pl.ds(pl.multiple_of(q * seqs, seqs), seqs), :]
+    masks = [own_mask[:, i : i + 1] for i in range(rows)]
+    for g in range(groups):
+        parts = [act[:, i, :] * masks[i] for i in range(g * pack, (g + 1) * pack)]
+        left_ref[:, g * 128 : (g + 1) * 128] = jnp.concatenate(
+            [p[:, :width] for p in parts], axis=1
+        ).astype(BF16)
+        right_ref[:, g * 128 : (g + 1) * 128] = jnp.concatenate(
+            [p[:, width:] for p in parts], axis=1
+        ).astype(BF16)
+    right_ref[...] = dot(right_ref[...], perm[...], 1, 0).astype(BF16)
     pl.semaphore_wait(barrier, count + 1)
 
     def plane_copy(src, dst, send, recv, peer_a, peer_q):
@@ -109,9 +147,16 @@
     for step in range(1, seq):
         left_copy(step).start()
 
+    mask_cols = dot(mask_all, col_pick, 1, 0).astype(BF16)
+    counts = dot(mask_cols, mask_rows[...].astype(BF16), 0, 0)
+    for copy in loads[4:]:
+        copy.wait()
+    own_pairs = dot(col_pick, pmask[...].astype(F32).astype(BF16), 0, 1)
+    scale = own_pairs / (counts + 0.001)
+    w_cd[...] = ow_ref[...].astype(F32).T
     for g in range(groups):
         parts = [
-            cot_ref[g * pack + k].astype(F32) * sct_ref[:, g * pack + k : g * pack + k + 1]
+            cot_ref[g * pack + k].astype(F32) * scale[:, g * pack + k : g * pack + k + 1]
             for k in range(pack)
         ]
         sg[g * cols : (g + 1) * cols, :] = jnp.concatenate(parts, axis=1).astype(BF16)
@@ -119,7 +164,7 @@
     lane_part = lax.broadcasted_iota(jnp.int32, (128, pack * chan), 1) // chan
     diagonal = (row_part == lane_part).astype(F32).astype(BF16)
     for d in range(width):
-        block = w_ref[d * width : (d + 1) * width, :]
+        block = w_cd[pl.ds(d, width, stride=width), :].astype(BF16)
         block = jnp.concatenate([block] * pack, axis=1)
         wbd[d * 128 : (d + 1) * 128, :] = jnp.concatenate([block] * pack, axis=0) * diagonal
     for ch in range(width // 8):
@@ -262,7 +307,7 @@
             i = g * pack + k
             pu_ref[i] = (
                 projected[g * cols : (g + 1) * cols, k * chan : (k + 1) * chan]
-                * sct_ref[:, i : i + 1]
+                * scale[:, i : i + 1]
             ).astype(BF16)
 
     left_sum = l2[q].astype(F32)
@@ -293,111 +338,107 @@
     for step in range(1, num):
         arrived(wrecv.at[step], wrsem.at[step])
         wo_sum = wo_sum + wrecv[step].astype(F32)
-    wo_ref[...] = wo_sum.astype(BF16)
+    wall[me] = wo_sum.astype(BF16)
+
+    def peer_copy(src, dst, send, recv, step):
+        peer = lax.rem(me + step, num)
+        return plane_copy(src, dst, send, recv, peer // seq, lax.rem(peer, seq))
+
+    def part_copy(step):
+        return peer_copy(wpart.at[h], inbox.at[step], psend.at[step], precv.at[step], step)
+
+    def wo_copy(step):
+        return peer_copy(wall.at[me], wall.at[me], asend.at[step], arecv.at[me], step)
+
+    for step in range(1, num):
+        wo_copy(step).start()
 
     final.wait_send()
     arrived(pair.at[other], crecv.at[2])
+    left_grad = jnp.concatenate([pair[0, 0], pair[1, 0]], axis=0).astype(F32)
+    right_grad = jnp.concatenate([pair[0, 1], pair[1, 1]], axis=0)
+    right_grad = dot(right_grad, perm[...], 1, 1)
+    for i in range(rows):
+        lanes = slice(i * width, (i + 1) * width)
+        act[:, i, :] = (
+            jnp.concatenate([left_grad[:, lanes], right_grad[:, lanes]], axis=1) * masks[i]
+        )
+    grads = act[...].reshape(seqs * rows, 2 * width).astype(BF16)
+
+    products = dot(grads, normed[...], 0, 0).astype(BF16)
     for core in range(2):
-        lg_ref[core * half : (core + 1) * half, :] = pair[core, 0]
-        rg_ref[core * half : (core + 1) * half, :] = pair[core, 1]
-
-    for step in range(1, dap):
-        right_copy(step).wait_send()
-    pl.when(jnp.logical_not(own))(lambda: right_copy(0).wait_send())
-    for step in range(1, seq):
-        left_copy(step).wait_send()
-    for step in range(1, num):
-        scatter(step).wait_send()
-    for dest_q in range(seq):
-
-        @pl.when(dest_q != q)
-        def _():
-            left_out(dest_q).wait_send()
-
-        for block in range(per):
-
-            @pl.when(jnp.logical_not(is_me(block, dest_q)))
-            def _():
-                right_out(block, dest_q).wait_send()
-
-
-def finish_kernel(
-    dap, seq, total_res, grads_ref, normed_ref, source_ref, weight_ref, wo_ref,
-    ga_ref, wl_ref, wr_ref, wog_ref,
-    part, inbox, sums, wall, send, recv, gsend, grecv, csend, crecv,
-):
-    num = dap * seq
-    width = wl_ref.shape[1]
-    chan = wog_ref.shape[1]
-    pack = 128 // width
-    h = lax.axis_index("chan")
-    other = 1 - h
-    me = lax.axis_index("dap") * seq + lax.axis_index("seq")
-    barrier, count = plane_barrier(dap, seq)
-    pl.semaphore_signal(barrier, inc=1, device_id={"chan": other}, device_id_type=MESH)
-    products = dot(grads_ref[...], normed_ref[...], 0, 0).astype(BF16)
-    for core in range(2):
-        part[core] = products[core * width : (core + 1) * width]
-    wall[me] = wo_ref[...]
-    pl.semaphore_wait(barrier, count + 1)
-
-    def plane_copy(src, dst, send_sem, recv_sem, step):
-        peer = lax.rem(me + step, num)
-        return pltpu.make_async_remote_copy(
-            src_ref=src, dst_ref=dst, send_sem=send_sem, recv_sem=recv_sem,
-            device_id={"dap": peer // seq, "seq": lax.rem(peer, seq)}, device_id_type=MESH,
-        )
-
-    def part_copy(step):
-        return plane_copy(part.at[h], inbox.at[step], send.at[step], recv.at[step], step)
-
-    def wo_copy(step):
-        return plane_copy(wall.at[me], wall.at[me], gsend.at[step], grecv.at[me], step)
-
+        wpart[core] = products[core * width : (core + 1) * width]
     for step in range(1, num):
         part_copy(step).start()
-    for step in range(1, num):
-        wo_copy(step).start()
-
-    values = source_ref[...].astype(F32)
-    center = values - jnp.mean(values, axis=-1, keepdims=True)
-    spread = lax.rsqrt(jnp.mean(center * center, axis=-1, keepdims=True) + 1e-05)
-    normal = center * spread
-    grad = dot(grads_ref[...], weight_ref[...], 1, 1)
-    along = jnp.mean(grad * normal, axis=-1, keepdims=True)
+    grad = dot(grads, both, 1, 0)
+    along = jnp.mean(grad * normal[...], axis=-1, keepdims=True)
     level = jnp.mean(grad, axis=-1, keepdims=True)
-    ga_ref[...] = (spread * (grad - level - normal * along)).astype(BF16)
-
-    inbox[0] = part[h]
-    for step in range(1, num):
-        part_copy(step).wait()
-    total = jnp.zeros(sums.shape[1:], F32)
-    for source in range(num):
-        total = total + inbox[lax.rem(me - source + num, num)].astype(F32)
-    sums[h] = total / total_res
-    exchange = pltpu.make_async_remote_copy(
-        src_ref=sums.at[h], dst_ref=sums.at[h], send_sem=csend, recv_sem=crecv,
-        device_id={"chan": other}, device_id_type=MESH,
+    ga_ref[...] = (
+        (spreads[...] * (grad - level - normal[...] * along))
+        .reshape(seqs, rows, chans)
+        .astype(BF16)
     )
-    exchange.start()
+
     for step in range(1, num):
         src = lax.rem(me + step, num)
-        arrived(wall.at[src], grecv.at[src])
+        arrived(wall.at[src], arecv.at[src])
     pieces = num * pack // width
     for ch in range(width // pack):
         tall = jnp.concatenate(
             [wall[ch * pieces + p].astype(F32) for p in range(pieces)], axis=0
         ).T / total_res
         for d in range(pack):
-            wog_ref[pl.ds(ch * pack + d, width, stride=width), :] = tall[
+            wtall[pl.ds(ch * pack + d, width, stride=width), :] = tall[
                 d * width : (d + 1) * width, :
             ]
+    wog_ref[...] = wtall[...].T
+
+    inbox[0] = wpart[h]
+    for step in range(1, num):
+        part_copy(step).wait()
+    total = jnp.zeros(sums.shape[1:], F32)
+    for source in range(num):
+        total = total + inbox[lax.rem(me - source + num, num)].astype(F32)
+    sums[h] = total / total_res
+    exchange = core_copy(sums.at[h], sums.at[h], 3)
+    exchange.start()
     exchange.wait_send()
-    arrived(sums.at[other], crecv)
-    wl_ref[...] = sums[0].T
-    wr_ref[...] = sums[1].T
+    arrived(sums.at[other], crecv.at[3])
+    wl_ref[...] = sums[0]
+    wr_ref[...] = sums[1]
+
     for step in range(1, num):
         wo_copy(step).wait_send()
+    for step in range(1, dap):
+        right_copy(step).wait_send()
+    pl.when(jnp.logical_not(own))(lambda: right_copy(0).wait_send())
+    for step in range(1, seq):
+        left_copy(step).wait_send()
+    for step in range(1, num):
+        scatter(step).wait_send()
+    for dest_q in range(seq):
+
+        @pl.when(dest_q != q)
+        def _():
+            left_out(dest_q).wait_send()
+
+        for block in range(per):
+
+            @pl.when(jnp.logical_not(is_me(block, dest_q)))
+            def _():
+                right_out(block, dest_q).wait_send()
+
+
+def store_kernel(*refs):
+    count = (len(refs) - 1) // 2
+    sems = refs[-1]
+    copies = [
+        pltpu.make_async_copy(refs[n], refs[count + n], sems.at[n]) for n in range(count)
+    ]
+    for copy in copies:
+        copy.start()
+    for copy in copies:
+        copy.wait()
 
 
 def body(alignment, align_mask, pair_mask, cotangent, left_weight, right_weight, out_weight):
@@ -408,26 +449,8 @@
     per, num = dap // seq, dap * seq
     total_res, all_seqs = rows * dap, seqs * seq
     cols = total_res // seq
-    a, q = lax.axis_index("dap"), lax.axis_index("seq")
     half = seqs // 2
     flat = rows * width
-
-    mask_bf = align_mask.astype(BF16)
-    own_mask = lax.dynamic_slice(align_mask, (q * seqs, a * rows), (seqs, rows)).astype(F32)
-    mask_rows = lax.dynamic_slice_in_dim(mask_bf, a * rows, rows, 1)
-    mask_cols = lax.dynamic_slice_in_dim(mask_bf, q * cols, cols, 1)
-    counts = dot(mask_cols, mask_rows, 0, 0)
-    own_pairs = lax.dynamic_slice_in_dim(pair_mask, q * cols, cols, 1)
-    scale_t = own_pairs.T.astype(F32) / (counts + 0.001)
-
-    normed = layer_norm(alignment.astype(F32)).astype(BF16).reshape(seqs * rows, chans)
-    both_weights = jnp.concatenate([left_weight, right_weight], axis=1)
-    act = dot(normed, both_weights, 1, 0)
-    act = (own_mask[:, :, None] * act.reshape(seqs, rows, 2 * width)).astype(BF16)
-    left = act[:, :, :width].reshape(seqs, flat)
-    right = act[:, :, width:].transpose(0, 2, 1).reshape(seqs, flat)
-    w_dc = out_weight.reshape(width, width, chan).transpose(1, 0, 2).reshape(width * width, chan)
-
     dma = pltpu.SemaphoreType.DMA
     shape = jax.ShapeDtypeStruct
     groups = rows // 4
@@ -436,15 +459,36 @@
     def room(*dims):
         return pltpu.VMEM(dims, BF16)
 
-    pair_update, lg, rg, wo = vmem_call(
-        functools.partial(pair_kernel, dap, seq),
-        (
-            shape((rows, cols, chan), BF16),
-            shape((seqs, flat), BF16),
-            shape((seqs, flat), BF16),
-            shape((wrows, 128), BF16),
-        ),
-        [
+    def wide(*dims):
+        return pltpu.VMEM(dims, F32)
+
+    args = (
+        alignment, align_mask, pair_mask, cotangent, left_weight.T, right_weight.T, out_weight.T,
+    )
+    out_shape = (
+        shape((rows, cols, chan), BF16),
+        shape((seqs, rows, chans), BF16),
+        shape((width, chans), F32),
+        shape((width, chans), F32),
+        shape((chan, width * width), F32),
+    )
+    results = pl.pallas_call(
+        functools.partial(whole_kernel, dap, seq, total_res),
+        out_shape=out_shape,
+        in_specs=[pl.BlockSpec(memory_space=pltpu.HBM)] * len(args),
+        out_specs=tuple(pl.BlockSpec(memory_space=pltpu.VMEM) for _ in out_shape),
+        scratch_shapes=[pltpu.VMEM(x.shape, x.dtype) for x in args]
+        + [
+            wide(seqs * rows, chans),
+            room(seqs * rows, chans),
+            wide(seqs * rows, 1),
+            wide(seqs, rows, 2 * width),
+            wide(all_seqs, rows),
+            wide(width * width, chan),
+            room(flat, flat),
+            room(seqs, flat),
+            room(seqs, flat),
+            wide(width * width, chan),
             room(groups * cols, 4 * chan),
             room(width * 128, 4 * chan),
             room(groups * cols, width * 128),
@@ -464,39 +508,31 @@
             room(dap, half, flat),
             room(2, 2, half, flat),
             room(num, wrows, 128),
+            room(2, width, chans),
+            room(num, width, chans),
+            wide(2, width, chans),
+            room(num, wrows, 128),
+            dma((7,)),
             dma((seq,)), dma((seq,)), dma((dap,)), dma((per, seq)),
-            dma((3,)), dma((3,)),
+            dma((4,)), dma((4,)),
             dma((seq,)), dma((seq,)),
             dma((per, seq)), dma((dap,)),
             dma((num,)), dma((num,)),
+            dma((num,)), dma((num,)),
+            dma((num,)), dma((num,)),
         ],
-        5,
-        0,
-    )(left, right, w_dc, cotangent, scale_t)
-
-    grads = jnp.concatenate(
-        [lg.reshape(seqs, rows, width), rg.reshape(seqs, width, rows).transpose(0, 2, 1)], axis=2
-    )
-    grads = (grads.astype(F32) * own_mask[:, :, None]).astype(BF16).reshape(seqs * rows, 2 * width)
-    grad_alignment, wl, wr, wog = vmem_call(
-        functools.partial(finish_kernel, dap, seq, total_res),
-        (
-            shape((seqs * rows, chans), BF16),
-            shape((chans, width), F32),
-            shape((chans, width), F32),
-            shape((width * width, chan), F32),
+        compiler_params=pltpu.CompilerParams(
+            vmem_limit_bytes=VMEM_BYTES, collective_id=0, has_side_effects=True
         ),
-        [
-            room(2, width, chans),
-            room(num, width, chans),
-            pltpu.VMEM((2, width, chans), F32),
-            room(num, wrows, 128),
-            dma((num,)), dma((num,)), dma((num,)), dma((num,)), dma, dma,
-        ],
-        5,
-        1,
-    )(grads, normed, alignment.reshape(seqs * rows, chans), both_weights, wo)
-    return pair_update, grad_alignment.reshape(seqs, rows, chans), wl, wr, wog
+    )(*args)
+    pair_update, grad_alignment, wl, wr, wog = pl.pallas_call(
+        store_kernel,
+        out_shape=out_shape,
+        in_specs=[pl.BlockSpec(memory_space=pl.ANY)] * len(results),
+        out_specs=tuple(pl.BlockSpec(memory_space=pltpu.HBM) for _ in out_shape),
+        scratch_shapes=[dma((len(results),))],
+    )(*results)
+    return pair_update, grad_alignment, wl.T, wr.T, wog.T
 
 
 def solution(mesh):

time: 48.1 us -> 65.2 us (1.36)
  Pallas kernels: 33.5 us -> 64.4 us
  local copies, waits for them, and re-layouts: 9.07 us -> 0 us
  other arithmetic: 3.64 us -> 0 us
    pallas_call x2, Pallas kernels: 33.5 us -> 64.4 us  [the longest x1 32.4 us: body(): pl.pallas_call(functools.partial(whole_kernel, dap, seq, total_res), out_...]
    unnamed x21 -> x0, local copies, waits for them, and re-layouts: 7.33 us -> none
    convert_element_type x4 -> x0, other arithmetic: 2.05 us -> none  [the longest x1 0.8 us: body(): lax.dynamic_slice(align_mask, (q * seqs, a * rows), (seqs, rows))]
    reduce_sum x2 -> x0, other arithmetic: 1.48 us -> none  [the longest x1 1.17 us: layer_norm(): center = values - jnp.mean(values, axis=-1, keepdims=True)]
    reshape x3 -> x0, local copies, waits for them, and re-layouts: 0.85 us -> none  [the longest x1 0.38 us: body(): rg.reshape(seqs, width, rows).transpose(0, 2, 1)]
where the time goes in v3:
time: 65.2 us; the launch traced here: 65 us
  Pallas kernels  64.4 us (99%)
    pallas_call x1, Pallas kernels, body(): pl.pallas_call(functools.partial(whole_kernel, dap, seq, total_res), out_...  32.4 us
    pallas_call x1, Pallas kernels, body(): pl.pallas_call(store_kernel, out_shape=out_shape, in_specs=[pl.BlockSpec(...  31.9 us

profile of v3, /device:TPU:0, one launch (start us, length us, event | category | flops | bytes accessed | tf_op | source)
XLA Modules:
  0.0 65.0 jit_solution(6447067610117356534)
XLA Ops:
  0.6 32.4 %shard_map.110 = (bf16[24,48,64]{2,1,0:T(8,128)(2,1)}, bf16[32,24,256]{2,1,0:T(8,128)(2,1)}, f32[32,256]{1,0:T(8,128)}, f32[32,256]{1,0:T(8,128)}, f32[64,1024]{1,0:T(8,128)}) custom-call(bf16[32,24,256]{2,1,0:T(8,128)(2,1)} %align_hbm.1, s32[64,96]{1,0:T(8,128)} %amask_hbm.1, s32[24,96]{1,0:T(8,128)} %pmask_hbm.1, bf16[24,48,64]{2,1,0:T(8,128)(2,1)} %cot_hbm.1, ...), custom_call_target="tpu_custom_call" | custom-call | tf_op jit(solution)/shard_map/pallas_call | solution.py:475
  33.1 31.9 %shard_map.111 = (bf16[24,48,64]{2,1,0:T(8,128)(2,1)}, bf16[32,24,256]{2,1,0:T(8,128)(2,1)}, f32[32,256]{1,0:T(8,128)}, f32[32,256]{1,0:T(8,128)}, f32[64,1024]{1,0:T(8,128)}) custom-call(bf16[24,48,64]{2,1,0:T(8,128)(2,1)} %get-tuple-element.15.refs_0_, bf16[32,24,256]{2,1,0:T(8,128)(2,1)} %get-tuple-element.16.refs_1_, ...), custom_call_target="tpu_custom_call" | custom-call | tf_op jit(solution)/shard_map/pallas_call | solution.py:528

commit v4 on v3

--- a/solution.py
+++ b/solution.py
@@ -430,14 +430,17 @@
 
 
 def store_kernel(*refs):
-    count = (len(refs) - 1) // 2
-    sems = refs[-1]
-    copies = [
-        pltpu.make_async_copy(refs[n], refs[count + n], sems.at[n]) for n in range(count)
-    ]
-    for copy in copies:
+    count = (len(refs) - 2) // 3
+    sources, dests, rooms = (refs[n * count : (n + 1) * count] for n in range(3))
+    in_sems, out_sems = refs[-2:]
+    ins = [pltpu.make_async_copy(sources[n], rooms[n], in_sems.at[n]) for n in range(count)]
+    outs = [pltpu.make_async_copy(rooms[n], dests[n], out_sems.at[n]) for n in range(count)]
+    for copy in ins:
         copy.start()
-    for copy in copies:
+    for n in range(count):
+        ins[n].wait()
+        outs[n].start()
+    for copy in outs:
         copy.wait()
 
 
@@ -528,9 +531,11 @@
     pair_update, grad_alignment, wl, wr, wog = pl.pallas_call(
         store_kernel,
         out_shape=out_shape,
-        in_specs=[pl.BlockSpec(memory_space=pl.ANY)] * len(results),
+        in_specs=[pl.BlockSpec(memory_space=pltpu.HBM)] * len(results),
         out_specs=tuple(pl.BlockSpec(memory_space=pltpu.HBM) for _ in out_shape),
-        scratch_shapes=[dma((len(results),))],
+        scratch_shapes=[pltpu.VMEM(x.shape, x.dtype) for x in out_shape]
+        + [dma((len(results),)), dma((len(results),))],
+        compiler_params=pltpu.CompilerParams(vmem_limit_bytes=VMEM_BYTES),
     )(*results)
     return pair_update, grad_alignment, wl.T, wr.T, wog.T
 

time: 65.2 us -> 35.3 us (0.54)
  Pallas kernels: 64.4 us -> 34.5 us
    pallas_call x1, Pallas kernels: 31.9 us -> 2.03 us  [body(): pl.pallas_call(store_kernel, out_shape=out_shape, in_specs=[pl.BlockSpec(...]
where the time goes in v4:
time: 35.3 us; the launch traced here: 35.1 us
  Pallas kernels  34.5 us (98%)
  between operations  0.64 us (2%)
    pallas_call x1, Pallas kernels, body(): pl.pallas_call(functools.partial(whole_kernel, dap, seq, total_res), out_...  32.4 us
    pallas_call x1, Pallas kernels, body(): pl.pallas_call(store_kernel, out_shape=out_shape, in_specs=[pl.BlockSpec(...  2.03 us

profile of v4, /device:TPU:0, one launch (start us, length us, event | category | flops | bytes accessed | tf_op | source)
XLA Modules:
  0.0 35.1 jit_solution(16879643138814751042)
XLA Ops:
  0.6 32.4 %shard_map.110 = (bf16[24,48,64]{2,1,0:T(8,128)(2,1)}, bf16[32,24,256]{2,1,0:T(8,128)(2,1)}, f32[32,256]{1,0:T(8,128)}, f32[32,256]{1,0:T(8,128)}, f32[64,1024]{1,0:T(8,128)}) custom-call(bf16[32,24,256]{2,1,0:T(8,128)(2,1)} %align_hbm.1, s32[64,96]{1,0:T(8,128)} %amask_hbm.1, s32[24,96]{1,0:T(8,128)} %pmask_hbm.1, bf16[24,48,64]{2,1,0:T(8,128)(2,1)} %cot_hbm.1, ...), custom_call_target="tpu_custom_call" | custom-call | tf_op jit(solution)/shard_map/pallas_call | solution.py:478
  33.1 2.0 %shard_map.111 = (bf16[24,48,64]{2,1,0:T(8,128)(2,1)}, bf16[32,24,256]{2,1,0:T(8,128)(2,1)}, f32[32,256]{1,0:T(8,128)}, f32[32,256]{1,0:T(8,128)}, f32[64,1024]{1,0:T(8,128)}) custom-call(bf16[24,48,64]{2,1,0:T(8,128)(2,1)} %get-tuple-element.15.refs_0_, bf16[32,24,256]{2,1,0:T(8,128)(2,1)} %get-tuple-element.16.refs_1_, ...), custom_call_target="tpu_custom_call" | custom-call | tf_op jit(solution)/shard_map/pallas_call | solution.py:531
